TPU v7x, 256 devices: a whole 4x4x8 slice. The times are simulated.
256 devices in a mesh: tm: 32 (over x, z), dp: 8 (over y, core).
Axes of the slice: x: 4, y: 4, z: 8, core: 2. Of those that a mesh axis runs over, the one named last changes fastest.
Arguments:
- features: float32 [8, 32, 32, 128], P('dp'), may hold values from -6 to 6
- cotangent: float32 [8, 32, 32, 128], P('dp'), may hold values from -6 to 6
- weights: bfloat16 [64, 9, 128, 128], P('tm'), may hold values from -0.1875 to 0.1875
- coarse_map: float32 [32, 128, 128], P('tm'), may hold values from -0.05 to 0.05
Outputs:
- boundary_states: float32 [32, 8, 32, 32, 128], P('tm', 'dp')
- adjoint_states: float32 [32, 8, 32, 32, 128], P('tm', 'dp')
- weight_grad: float32 [64, 9, 128, 128], P('tm')
All inputs are finite; a program needn't handle non-finite values.
Results may differ from a plain program's by a relative error of at most 0.0045.
Values sent between devices are 32-bit elements; how exact they have to be, the bound alone decides.
A program may use at most 128 MiB of HBM per device.

v0:
```python
import jax
import jax.numpy as jnp
from jax import lax
from jax.sharding import PartitionSpec as P

CYCLES = 2


step_size = 0.25
coarse_diagonal = 0.9


def carried_in(shard, axis, combine, identity, reverse):
    count, position = (lax.axis_size(axis), lax.axis_index(axis))
    everything = jax.tree.map(lambda part: lax.all_gather(part, axis), shard)
    start = jax.tree.map(
        lambda part, zero: jnp.broadcast_to(jnp.asarray(zero, part.dtype), part.shape),
        shard,
        identity,
    )

    def turn(k, before):
        at = count - 1 - k if reverse else k
        reached = at > position if reverse else at < position
        new = combine(before, jax.tree.map(lambda part: part[at], everything))
        return jax.tree.map(lambda a, b: jnp.where(reached, a, b), new, before)

    return lax.fori_loop(0, count, turn, start)


def from_behind(shard, axis, by):
    count = lax.axis_size(axis)
    pairs = [(i, i + by) for i in range(count) if 0 <= i + by < count]
    return lax.ppermute(shard, axis, pairs)


def pad_map(values):
    return jnp.pad(values, ((0, 0), (1, 1), (1, 1), (0, 0)))


def tap_slices(padded, height, breadth, flipped):
    pieces = []
    for tap_index in range(9):
        tap_row = tap_index // 3
        tap_col = tap_index % 3
        if flipped:
            tap_row = 2 - tap_row
            tap_col = 2 - tap_col
        pieces.append(padded[:, tap_row : tap_row + height, tap_col : tap_col + breadth, :])
    return pieces


def convolve(active, kernel):
    images, height, breadth, channels = active.shape
    summed = jnp.zeros((images * height * breadth, kernel.shape[2]), jnp.float32)
    for tap_index, piece in enumerate(tap_slices(pad_map(active), height, breadth, False)):
        summed = summed + jnp.dot(
            piece.reshape(-1, channels), kernel[tap_index], preferred_element_type=jnp.float32
        )
    return summed.reshape(images, height, breadth, -1)


def convolve_back(signal, kernel):
    images, height, breadth, channels = signal.shape
    summed = jnp.zeros((images * height * breadth, kernel.shape[1]), jnp.float32)
    for tap_index, piece in enumerate(tap_slices(pad_map(signal), height, breadth, True)):
        summed = summed + jnp.dot(
            piece.reshape(-1, channels), kernel[tap_index].T, preferred_element_type=jnp.float32
        )
    return summed.reshape(images, height, breadth, -1)


def kernel_grad(active, signal):
    images, height, breadth, channels = active.shape
    flat_signal = signal.reshape(-1, signal.shape[3])
    blocks = []
    for piece in tap_slices(pad_map(active), height, breadth, False):
        blocks.append(
            lax.dot_general(
                piece.reshape(-1, channels),
                flat_signal,
                (((0,), (0,)), ((), ())),
                preferred_element_type=jnp.float32,
            )
        )
    return jnp.stack(blocks, 0)


def forward_step(current, kernel):
    return current + step_size * convolve(jnp.tanh(current).astype(jnp.bfloat16), kernel)


def adjoint_step(current, signal, kernel):
    active = jnp.tanh(current)
    return signal + step_size * (1.0 - active * active) * convolve_back(
        signal.astype(jnp.bfloat16), kernel
    )


def apply_map(vector, matrix):
    flat = jnp.dot(
        vector.reshape(-1, vector.shape[-1]),
        matrix,
        precision=lax.Precision.HIGHEST,
        preferred_element_type=jnp.float32,
    )
    return flat.reshape(vector.shape)


def compose(earlier, later):
    matrix = jnp.dot(
        earlier[0], later[0], precision=lax.Precision.HIGHEST, preferred_element_type=jnp.float32
    )
    return (matrix, apply_map(earlier[1], later[0]) + later[1])


def sweep_scan(residual, matrix, backward):
    identity = jnp.eye(matrix.shape[0], dtype=jnp.float32)
    prefix = carried_in(
        (matrix, residual), "tm", compose, (identity, jnp.zeros_like(residual)), backward
    )
    return apply_map(prefix[1], matrix) + residual


def local(features, cotangent, weights, coarse_map):
    devices = lax.axis_size("tm")
    position = lax.axis_index("tm")
    channels = features.shape[3]
    layers_dev = weights.shape[0]
    at_first = position == 0
    at_final = position == devices - 1
    forward_map = coarse_diagonal * jnp.eye(channels, dtype=jnp.float32) + coarse_map[0]
    backward_map = forward_map.T

    def correction(residual, backward):
        if backward:
            return sweep_scan(residual, backward_map, True)
        return sweep_scan(residual, forward_map, False)

    def relax_forward(ends):
        incoming = from_behind(ends, "tm", 1)
        current = jnp.where(at_first, features, incoming)
        states = []
        for layer_index in range(layers_dev):
            states.append(current)
            current = forward_step(current, weights[layer_index])
        return (current, states)

    ends = features
    for cycle_index in range(CYCLES):
        propagated, _ = relax_forward(ends)
        ends = ends + correction(propagated - ends, False)
    _, states = relax_forward(ends)

    def adjoint_start(adjoint):
        incoming = from_behind(adjoint, "tm", -1)
        return jnp.where(at_final, cotangent, incoming)

    adjoint = cotangent
    for cycle_index in range(CYCLES):
        current = adjoint_start(adjoint)
        for layer_index in reversed(range(layers_dev)):
            current = adjoint_step(states[layer_index], current, weights[layer_index])
        adjoint = adjoint + correction(current - adjoint, True)
    factor = step_size / (features.shape[0] * lax.axis_size("dp"))
    current = adjoint_start(adjoint)
    gradients = [None] * layers_dev
    for layer_index in reversed(range(layers_dev)):
        local_grad = kernel_grad(
            jnp.tanh(states[layer_index]).astype(jnp.bfloat16), current.astype(jnp.bfloat16)
        )
        gradients[layer_index] = local_grad
        if layer_index > 0:
            current = adjoint_step(states[layer_index], current, weights[layer_index])
    stacked = jnp.stack(gradients, 0)
    stacked = lax.psum(stacked, "dp") * factor
    return (ends[None], adjoint[None], stacked)


def solution(mesh):
    placed = (
        P("dp", None, None, None),
        P("dp", None, None, None),
        P("tm", None, None, None),
        P("tm", None, None),
    )
    return jax.shard_map(
        local,
        mesh=mesh,
        in_specs=placed,
        out_specs=(
            P("tm", "dp", None, None, None),
            P("tm", "dp", None, None, None),
            P("tm", None, None, None),
        ),
        check_vma=False,
    )
```

profile of v0, /device:TPU:1, one launch (start us, length us, event | category | flops | bytes accessed | tf_op | source)
XLA Modules:
  0.0 1216.6 jit_solution(15981356654745614103)
XLA Ops:
  7.2 4.5 collective-permute-start
  13.3 9.3 collective-permute-done
  30.0 59.7 %all-gather.12.cloned.1.call-done = f32[32,128,128]{2,1,0:T(8,128)} async-done(((f32[1,128,128]{2,1,0:T(8,128)}), f32[32,128,128]{2,1,0:T(8,128)}) %all-gather.12.cloned.1.call-update) | async-done | bytes 2097168 | tf_op jit(solution)/shard_map/all_gather | solution.py:15
  89.8 144.5 %all-gather.14.cloned.1.call-done = f32[32,32,32,128]{3,2,1,0:T(8,128)} async-done(((f32[1,32,32,128]{3,2,1,0:T(8,128)}), f32[32,32,32,128]{3,2,1,0:T(8,128)}) %all-gather.14.cloned.1.call-update) | async-done | bytes 16777232 | tf_op jit(solution)/shard_map/all_gather | solution.py:15
  234.2 99.0 %while.60 = (s32[]{:T(128)}, f32[1,32,32,128]{3,2,1,0:T(8,128)S(1)}, s32[]{:T(128)}, f32[32,128,128]{2,1,0:T(8,128)}, f32[32,1,32,32,128]{4,3,2,1,0:T(8,128)}, /*index=5*/s32[]{:T(128)}, s32[]{:T(128)}) while((s32[]{:T(128)}, f32[1,32,32,128]{3,2,1,0:T(8,128)S(1)}, s32[]{:T(128)}, f32[32,128,128]{2,1,0:T(8,128)}, ...), condition=%wide.region_1.2_spmd.clone, body=%wide.region_0.1_spmd.clone.sunk | while | flops 201850880 | bytes 5308530 | solution.py:28
  234.3 1.5 convolution_bitcast_fusion.30
  240.5 1.5 convolution_bitcast_fusion.30
  243.6 1.5 convolution_bitcast_fusion.30
  249.8 1.5 convolution_bitcast_fusion.30
  259.1 1.5 convolution_bitcast_fusion.30
  268.3 1.5 convolution_bitcast_fusion.30
  277.6 1.5 convolution_bitcast_fusion.30
  286.9 1.5 convolution_bitcast_fusion.30
  296.2 1.5 convolution_bitcast_fusion.30
  305.5 1.5 convolution_bitcast_fusion.30
  314.7 1.5 convolution_bitcast_fusion.30
  324.0 1.5 convolution_bitcast_fusion.30
  335.3 10.1 collective-permute-done.1
  353.3 12.3 %collective-permute-done.2 = f32[1,32,32,128]{3,2,1,0:T(8,128)S(1)} collective-permute-done((f32[1,32,32,128]{3,2,1,0:T(8,128)S(1)}, f32[1,32,32,128]{3,2,1,0:T(8,128)S(1)}, u32[]{:S(2)}, u32[]{:S(2)}) %collective-permute-start.2) | collective-permute-done | bytes 524320 | tf_op jit(solution)/shard_map/ppermute | solution.py:34
  369.0 124.8 %all-gather.16.cloned.1.call-done = f32[32,32,32,128]{3,2,1,0:T(8,128)} async-done(((f32[1,32,32,128]{3,2,1,0:T(8,128)}), f32[32,32,32,128]{3,2,1,0:T(8,128)}) %all-gather.16.cloned.1.call-update) | async-done | bytes 16777232 | tf_op jit(solution)/shard_map/all_gather | solution.py:15
  493.8 98.9 %while.61 = (s32[]{:T(128)}, f32[1,32,32,128]{3,2,1,0:T(8,128)S(1)}, s32[]{:T(128)}, f32[32,128,128]{2,1,0:T(8,128)}, f32[32,1,32,32,128]{4,3,2,1,0:T(8,128)}, /*index=5*/s32[]{:T(128)}, s32[]{:T(128)}) while((s32[]{:T(128)}, f32[1,32,32,128]{3,2,1,0:T(8,128)S(1)}, s32[]{:T(128)}, f32[32,128,128]{2,1,0:T(8,128)}, ...), condition=%wide.region_3.4_spmd.clone, body=%wide.region_2.3_spmd.clone.sunk | while | flops 201850880 | bytes 5308530 | solution.py:28
  503.1 1.5 convolution_bitcast_fusion.31
  506.2 1.5 convolution_bitcast_fusion.31
  509.3 1.5 convolution_bitcast_fusion.31
  518.6 1.5 convolution_bitcast_fusion.31
  521.7 1.5 convolution_bitcast_fusion.31
  540.2 1.5 convolution_bitcast_fusion.31
  543.3 1.5 convolution_bitcast_fusion.31
  546.4 1.5 convolution_bitcast_fusion.31
  552.6 1.5 convolution_bitcast_fusion.31
  555.7 1.5 convolution_bitcast_fusion.31
  558.8 1.5 convolution_bitcast_fusion.31
  561.9 1.5 convolution_bitcast_fusion.31
  592.8 1.9 fusion.27
  594.7 1.7 collective-permute-start.3
  597.1 9.2 collective-permute-done.3
  613.5 2.9 copy.31
  616.4 139.5 %all-gather.20.cloned.1.call-done = f32[32,32,32,128]{3,2,1,0:T(8,128)} async-done(((f32[1,32,32,128]{3,2,1,0:T(8,128)}), f32[32,32,32,128]{3,2,1,0:T(8,128)}) %all-gather.20.cloned.1.call-update) | async-done | bytes 16777232 | tf_op jit(solution)/shard_map/all_gather | solution.py:15
  755.9 99.1 %while.62 = (s32[]{:T(128)}, f32[1,32,32,128]{3,2,1,0:T(8,128)S(1)}, s32[]{:T(128)}, f32[32,128,128]{2,1,0:T(8,128)}, f32[32,1,32,32,128]{4,3,2,1,0:T(8,128)}, /*index=5*/s32[]{:T(128)}, s32[]{:T(128)}, s32[]{:T(128)}, s32[]{:T(128)}) while((s32[]{:T(128)}, f32[1,32,32,128]{3,2,1,0:T(8,128)S(1)}, s32[]{:T(128)}, ...), condition=%wide.region_5.6_spmd.clone, body=%wide.region_4.5_spmd.clone.sunk | while | flops 201850880 | bytes 5308592 | solution.py:28
  855.0 1.7 fusion.29
  858.0 13.0 %collective-permute-done.4 = f32[1,32,32,128]{3,2,1,0:T(8,128)S(1)} collective-permute-done((f32[1,32,32,128]{3,2,1,0:T(8,128)S(1)}, f32[1,32,32,128]{3,2,1,0:T(8,128)S(1)}, u32[]{:S(2)}, u32[]{:S(2)}) %collective-permute-start.4) | collective-permute-done | bytes 524320 | tf_op jit(solution)/shard_map/ppermute | solution.py:34
  877.7 139.7 %all-gather.22.cloned.1.call-done = f32[32,32,32,128]{3,2,1,0:T(8,128)} async-done(((f32[1,32,32,128]{3,2,1,0:T(8,128)}), f32[32,32,32,128]{3,2,1,0:T(8,128)}) %all-gather.22.cloned.1.call-update) | async-done | bytes 16777232 | tf_op jit(solution)/shard_map/all_gather | solution.py:15
  1017.4 99.1 %while.63 = (s32[]{:T(128)}, f32[1,32,32,128]{3,2,1,0:T(8,128)S(1)}, s32[]{:T(128)}, f32[32,128,128]{2,1,0:T(8,128)}, f32[32,1,32,32,128]{4,3,2,1,0:T(8,128)}, /*index=5*/s32[]{:T(128)}, s32[]{:T(128)}, s32[]{:T(128)}, s32[]{:T(128)}) while((s32[]{:T(128)}, f32[1,32,32,128]{3,2,1,0:T(8,128)S(1)}, s32[]{:T(128)}, ...), condition=%wide.region_7.8_spmd.clone, body=%wide.region_6.7_spmd.clone.sunk | while | flops 201850880 | bytes 5308592 | solution.py:28
  1116.5 1.8 fusion.31
  1118.3 1.6 collective-permute-start.5
  1120.0 12.8 %collective-permute-done.5 = f32[1,32,32,128]{3,2,1,0:T(8,128)S(1)} collective-permute-done((f32[1,32,32,128]{3,2,1,0:T(8,128)S(1)}, f32[1,32,32,128]{3,2,1,0:T(8,128)S(1)}, u32[]{:S(2)}, u32[]{:S(2)}) %collective-permute-start.5) | collective-permute-done | bytes 524320 | tf_op jit(solution)/shard_map/ppermute | solution.py:34
  1141.7 65.7 %all-reduce.13.cloned.1.call-done = f32[2,9,128,128]{3,2,1,0:T(8,128)} async-done(((f32[2,9,128,128]{3,2,1,0:T(8,128)}), f32[2,9,128,128]{3,2,1,0:T(8,128)}) %all-reduce.13.cloned.1.call-update) | async-done | bytes 1179664 | tf_op jit(solution)/shard_map/psum | solution.py:176
  1207.4 2.4 broadcast_multiply_fusion
  (682 shorter events, 399.4 us)
Async XLA Ops:
  7.2 16.9 %copy-start.2 = (bf16[2,9,128,128]{3,2,1,0:T(8,128)(2,1)S(1)}, bf16[2,9,128,128]{3,2,1,0:T(8,128)(2,1)}, u32[]{:S(2)}) copy-start(bf16[2,9,128,128]{3,2,1,0:T(8,128)(2,1)} %param.14) | copy-start | bytes 1769476
  7.2 82.6 %all-gather.12.cloned.1.call-start = ((), (), s32[]{:S(2)}) async-start(), calls=%async_computation | async-start | bytes 2162688 | tf_op jit(solution)/shard_map/all_gather | solution.py:15
  7.2 15.4 %collective-permute-start = (f32[1,32,32,128]{3,2,1,0:T(8,128)}, f32[1,32,32,128]{3,2,1,0:T(8,128)S(1)}, u32[]{:S(2)}, u32[]{:S(2)}) collective-permute-start(f32[1,32,32,128]{3,2,1,0:T(8,128)} %param.12), channel_id=1, source_target_pairs={{0,8},{8,16},{16,24},{24,32},{32,40},{40,48},{48,56},{56,64},{64,7... | collective-permute-start | bytes 1572872 | tf_op jit(solution)/shard_map/ppermute | solution.py:34
  13.3 220.9 %all-gather.14.cloned.1.call-start = ((), (), s32[]{:S(2)}) async-start(), calls=%async_computation.2 | async-start | bytes 17301504 | tf_op jit(solution)/shard_map/all_gather | solution.py:15
  25.4 1.0 copy-start.1
  30.0 463.9 %all-gather.16.cloned.1.call-start = ((), (), s32[]{:S(2)}) async-start(), calls=%async_computation.3 | async-start | bytes 17301504 | tf_op jit(solution)/shard_map/all_gather | solution.py:15
  234.2 99.0 %copy-start.8 = (f32[1,32,32,128]{3,2,1,0:T(8,128)S(1)}, f32[1,32,32,128]{3,2,1,0:T(8,128)}, u32[]{:S(2)}) copy-start(f32[1,32,32,128]{3,2,1,0:T(8,128)} %add_subtract_fusion.3) | copy-start | bytes 1572868
  234.2 99.0 %copy-start.10 = (f32[1,128,128]{2,1,0:T(8,128)S(1)}, f32[1,128,128]{2,1,0:T(8,128)}, u32[]{:S(2)}) copy-start(f32[1,128,128]{2,1,0:T(8,128)} %param.15) | copy-start | bytes 196612
  333.8 16.4 %copy-start.9 = (f32[1,32,32,128]{3,2,1,0:T(8,128)}, f32[1,32,32,128]{3,2,1,0:T(8,128)S(1)}, u32[]{:S(2)}) copy-start(f32[1,32,32,128]{3,2,1,0:T(8,128)S(1)} %fusion.25) | copy-start | bytes 1572868
  333.9 11.6 collective-permute-start.1
  350.1 1.3 copy-start
  351.3 262.2 %all-gather.18.cloned.1.call-start = ((), (), s32[]{:S(2)}) async-start(), calls=%async_computation.4 | async-start | bytes 2162688 | tf_op jit(solution)/shard_map/all_gather | solution.py:15
  351.3 14.4 %collective-permute-start.2 = (f32[1,32,32,128]{3,2,1,0:T(8,128)S(1)}, f32[1,32,32,128]{3,2,1,0:T(8,128)S(1)}, u32[]{:S(2)}, u32[]{:S(2)}) collective-permute-start(f32[1,32,32,128]{3,2,1,0:T(8,128)S(1)} %copy-done), channel_id=1, source_target_pairs={{8,0},{16,8},{24,16},{32,24},{40,32},{48,40},{56,48},{64,56},{72,6... | collective-permute-start | bytes 1572872 | tf_op jit(solution)/shard_map/ppermute | solution.py:34
  353.3 402.6 %all-gather.20.cloned.1.call-start = ((), (), s32[]{:S(2)}) async-start(), calls=%async_computation.5 | async-start | bytes 17301504 | tf_op jit(solution)/shard_map/all_gather | solution.py:15
  365.7 1.4 copy-start.5
  592.8 3.6 copy-start.11
  592.8 3.6 copy-start.13
  592.8 3.8 copy-start.12
  594.6 2.4 copy-start.14
  594.7 11.6 collective-permute-start.3
  606.4 5.8 copy-start.3
  608.3 1.3 copy-start.6
  613.4 404.0 %all-gather.22.cloned.1.call-start = ((), (), s32[]{:S(2)}) async-start(), calls=%async_computation.6 | async-start | bytes 17301504 | tf_op jit(solution)/shard_map/all_gather | solution.py:15
  856.7 19.5 %copy-start.7 = (f32[1,32,32,128]{3,2,1,0:T(8,128)}, f32[1,32,32,128]{3,2,1,0:T(8,128)S(1)}, u32[]{:S(2)}) copy-start(f32[1,32,32,128]{3,2,1,0:T(8,128)S(1)} %fusion.29) | copy-start | bytes 1572868
  856.7 14.3 %collective-permute-start.4 = (f32[1,32,32,128]{3,2,1,0:T(8,128)S(1)}, f32[1,32,32,128]{3,2,1,0:T(8,128)S(1)}, u32[]{:S(2)}, u32[]{:S(2)}) collective-permute-start(f32[1,32,32,128]{3,2,1,0:T(8,128)S(1)} %fusion.29), channel_id=1, source_target_pairs={{8,0},{16,8},{24,16},{32,24},{40,32},{48,40},{56,48},{64,56},{72,6... | collective-permute-start | bytes 1572872 | tf_op jit(solution)/shard_map/ppermute | solution.py:34
  875.5 1.0 copy-start.4
  877.6 329.7 %all-reduce.13.cloned.1.call-start = ((), (), s32[]{:S(2)}) async-start(), calls=%async_computation.1 | async-start | bytes 2359296 | tf_op jit(solution)/shard_map/psum | solution.py:176
  1118.3 15.2 %copy-start.15 = (f32[1,32,32,128]{3,2,1,0:T(8,128)}, f32[1,32,32,128]{3,2,1,0:T(8,128)S(1)}, u32[]{:S(2)}) copy-start(f32[1,32,32,128]{3,2,1,0:T(8,128)S(1)} %fusion.31) | copy-start | bytes 1572868
  1118.3 14.9 %copy-start.16 = (bf16[1,32,32,128]{3,2,1,0:T(8,128)(2,1)S(1)}, bf16[1,32,32,128]{3,2,1,0:T(8,128)(2,1)}, u32[]{:S(2)}) copy-start(bf16[1,32,32,128]{3,2,1,0:T(8,128)(2,1)} %get-tuple-element.631) | copy-start | bytes 786436
  1118.3 14.4 %collective-permute-start.5 = (f32[1,32,32,128]{3,2,1,0:T(8,128)S(1)}, f32[1,32,32,128]{3,2,1,0:T(8,128)S(1)}, u32[]{:S(2)}, u32[]{:S(2)}) collective-permute-start(f32[1,32,32,128]{3,2,1,0:T(8,128)S(1)} %fusion.31), channel_id=1, source_target_pairs={{8,0},{16,8},{24,16},{32,24},{40,32},{48,40},{56,48},{64,56},{72,6... | collective-permute-start | bytes 1572872 | tf_op jit(solution)/shard_map/ppermute | solution.py:34
Sparse Core Ops, SparseCore 0:
  13.4 76.3 all-gather.11
  92.9 141.2 all-gather.13
  351.4 142.3 all-gather.15
  496.1 69.1 all-gather.17
  613.5 142.3 all-gather.19
  877.7 139.5 all-gather.21
  1141.8 65.5 all-reduce.12
where the time goes:
time: 1230 us; the launch traced here: 1220 us
  waiting for transfers between devices  741 us (60%)
  matrix products  222 us (18%)
  other arithmetic  187 us (15%)
  local copies, waits for them, and re-layouts  32 us (3%)
  between operations  15.4 us (1%)
    all_gather x6, waiting for transfers between devices, carried_in(): everything = jax.tree.map(lambda part: lax.all_gather(part, axis), shard)  608 us
    dot_general x132, matrix products, apply_map(): jnp.dot(vector.reshape(-1, vector.shape[-1]), matrix, precision=lax.Preci...  197 us
    select_n x128, other arithmetic, turn(): return jax.tree.map(lambda a, b: jnp.where(reached, a, b), new, before)  169 us
    ppermute x6, waiting for transfers between devices, from_behind(): return lax.ppermute(shard, axis, pairs)  66.7 us
    psum x1, waiting for transfers between devices, local(): stacked = lax.psum(stacked, 'dp') * factor  65.7 us
  transfers between devices with their start and end apart: 13, of which 12 were waited for; matrix products, arithmetic and copies ran while one was open for 10% of the time, Pallas kernels for 0%

commit v1 on v0

v1 whole, which is shorter than its diff:
```python
import functools

import jax
import jax.numpy as jnp
from jax import lax
from jax.experimental import pallas as pl
from jax.experimental.pallas import tpu as pltpu
from jax.sharding import PartitionSpec as P

MESH = pl.DeviceIdType.MESH
STEP = 0.25
DIAGONAL = 0.9
SIDE = 32
PIXELS = SIDE * SIDE
CH = 128
BANDS = 2
EDGES = ((0, 22, 32), (0, 20, 32), (0, 18, 32), (0, 16, 32))
TAPS = 9 * CH
F32, BF16 = jnp.float32, jnp.bfloat16


def two_terms(value):
    high = value.astype(BF16)
    return high, (value - high.astype(F32)).astype(BF16)


def times(value, tile):
    high, low = two_terms(value)
    both = jnp.dot(jnp.concatenate([high, low], 1), tile, preferred_element_type=F32)
    return both[:, :CH] + both[:, CH:]


def split(first, last, most=10):
    count = -(-(last - first) // most)
    cuts = [first + (last - first) * n // count for n in range(count + 1)]
    return list(zip(cuts[:-1], cuts[1:]))


def body(
    NX, NZ, NY, NC, factor,
    feat_in, cot_in, w_in, cm_in,
    ends, adj, grad,
    feat, cot, w, cm,
    x3a, x3b, z3a, z3b, wt, start, mid, prop, d0, d1, ycot, zt, zt0,
    resout, resin, eout, ein, tin, gin, pin, prods, temps, maps, segs, local_grad, gs, hsum, yin,
    in_s,
    res_s, res_r, e_s, e_r, t_s, t_r, g_s, g_r, gf_s, gf_r, p_s, p_r, sib_s, sib_r, rs_s, rs_r, ag_s, ag_r, fw_s, fw_r,
):
    loads = [
        pltpu.make_async_copy(src, dst, in_s.at[n])
        for n, (src, dst) in enumerate(((cm_in, cm), (feat_in, feat), (w_in, w), (cot_in, cot)))
    ]
    for load in loads:
        load.start()

    tm, dp = lax.axis_index("tm"), lax.axis_index("dp")
    x, z = tm // NZ, lax.rem(tm, NZ)
    y, c = dp // NC, lax.rem(dp, NC)
    half = TAPS // NC
    part = half // NY
    far_first = sorted(range(1, NZ), key=lambda d: -min(d, NZ - d))

    def to_z(d):
        return {"tm": x * NZ + lax.rem(z + d, NZ)}

    def to_x(d):
        return {"tm": lax.rem(x + d, NX) * NZ + z}

    def to_y(d):
        return {"dp": lax.rem(y + d, NY) * NC + c}

    def to_core():
        return {"dp": y * NC + (NC - 1 - c)}

    def remote(src, dst, send, recv, device):
        return pltpu.make_async_remote_copy(
            src_ref=src, dst_ref=dst, send_sem=send, recv_sem=recv, device_id=device, device_id_type=MESH
        )

    def each(count, f, first=0):
        def go(i, carry):
            f(i)
            return carry
        lax.fori_loop(first, count, go, 0)

    barrier = pltpu.get_barrier_semaphore()

    def greet(device):
        pl.semaphore_signal(barrier, inc=1, device_id=device, device_id_type=MESH)

    each(NZ, lambda d: greet(to_z(d)), 1)
    each(NX, lambda d: greet(to_x(d)), 1)
    each(NY, lambda d: greet(to_y(d)), 1)
    greet(to_core())

    def px(first, last):
        return slice(first * SIDE, last * SIDE)

    def fill(buffer, first, last, value):
        size = (last - first) * SIDE
        column = lax.rem(lax.broadcasted_iota(jnp.int32, (size, CH), 0), SIDE)
        left = jnp.where(column == 0, 0.0, pltpu.roll(value, 1, 0))
        right = jnp.where(column == SIDE - 1, 0.0, pltpu.roll(value, size - 1, 0))
        at = px(first + 1, last + 1)
        buffer[at, :CH] = left.astype(BF16)
        buffer[at, CH : 2 * CH] = value.astype(BF16)
        buffer[at, 2 * CH :] = right.astype(BF16)

    def conv(buffer, first, last, kernel):
        pieces = [buffer[px(first + r, last + r), :] for r in range(3)]
        return jnp.dot(jnp.concatenate(pieces, 1), kernel, preferred_element_type=F32)

    zero_row = jnp.zeros((SIDE, 3 * CH), BF16)
    for buffer in (x3a, x3b, z3a, z3b):
        buffer[:SIDE, :] = zero_row
        buffer[PIXELS + SIDE :, :] = zero_row
    eye = (lax.broadcasted_iota(jnp.int32, (CH, CH), 0) == lax.broadcasted_iota(jnp.int32, (CH, CH), 1)).astype(F32)
    loads[0].wait()
    gin[z] = DIAGONAL * eye + cm[...]

    loads[1].wait()
    for p, q in split(0, SIDE):
        value = feat[px(p, q), :]
        start[px(p, q), :] = value
        fill(x3a, p, q, jnp.tanh(value))
    loads[2].wait()
    pl.semaphore_wait(barrier, NZ - 1 + NX - 1 + NY - 1 + 1)

    gh = pl.ds(pl.multiple_of(c * (CH // NC), CH // NC), CH // NC)

    def g_copy(d):
        return remote(gin.at[z, gh], gin.at[z, gh], g_s.at[d], g_r.at[d], to_z(d))

    def g_forward(d):
        zs = lax.rem(z + NZ - d, NZ)
        return remote(gin.at[zs, gh], gin.at[zs, gh], gf_s.at[d], gf_r.at[d], to_core())

    for d in far_first:
        g_copy(d).start()

    def share(k, b):
        first, last = EDGES[k][b], EDGES[k][b + 1]
        return first * SIDE, (last - first) * SIDE // NZ

    def spot(k, b, n):
        base, R = share(k, b)
        if isinstance(n, int):
            return slice(base + n * R, base + n * R + R)
        return pl.ds(pl.multiple_of(base + n * R, 8), R)

    def res_copy(k, b, d):
        zp = lax.rem(z + d, NZ)
        m = BANDS * k + b
        return remote(
            resout.at[k, spot(k, b, zp)], resin.at[k, spot(k, b, z)], res_s.at[m, d], res_r.at[m, d], to_z(d)
        )

    def send_residual(k, b):
        for d in far_first:
            res_copy(k, b, d).start()
        resin[k, spot(k, b, z), :] = resout[k, spot(k, b, z), :]

    def t_spot(k, b):
        base, R = share(k, b)
        return slice(base // NZ, base // NZ + R)

    def t_copy(k, b, d):
        m = BANDS * k + b
        at = t_spot(k, b)
        return remote(tin.at[k, x, at], tin.at[k, x, at], t_s.at[m, d], t_r.at[m, d], to_x(d))

    def e_copy(k, b, d):
        zp = lax.rem(z + d, NZ)
        m = BANDS * k + b
        return remote(eout.at[k, spot(k, b, zp)], ein.at[k, spot(k, b, z)], e_s.at[m, d], e_r.at[m, d], to_z(d))

    def put(where, index, matrix):
        high, low = two_terms(matrix)
        where[(*index, slice(0, CH), slice(0, CH))] = high
        where[(*index, slice(0, CH), slice(CH, None))] = low
        where[(*index, slice(CH, None), slice(0, CH))] = high
        where[(*index, slice(CH, None), slice(CH, None))] = jnp.zeros((CH, CH), BF16)

    def scan(k, b, backward):
        total_kind, chain_kind, carry_kind = (3, 1, 5) if backward else (4, 0, 2)
        at = t_spot(k, b)
        edge = NZ - 1 if backward else 0
        for d in far_first[::-1]:
            res_copy(k, b, d).wait_recv()
        inner = NZ - 1 - edge
        total = resin[k, spot(k, b, inner), :]
        for s in range(NZ):
            if s != inner:
                total = total + times(resin[k, spot(k, b, s), :], maps[total_kind, s + (0 if backward else 1)])
        tin[k, x, at, :] = total
        for d in range(1, NX):
            t_copy(k, b, d).start()
        run = {}
        if backward:
            value = resin[k, spot(k, b, NZ - 1), :]
            run[NZ - 2] = value
            for s in range(NZ - 2, 0, -1):
                value = times(value, maps[chain_kind, s]) + resin[k, spot(k, b, s), :]
                run[s - 1] = value
        else:
            value = resin[k, spot(k, b, 0), :]
            run[1] = value
            for s in range(1, NZ - 1):
                value = times(value, maps[chain_kind, s]) + resin[k, spot(k, b, s), :]
                run[s + 1] = value
        for n in run:
            eout[k, spot(k, b, n), :] = run[n]
        if (k, b) == (0, 0):
            segments_arrive()
        for d in range(1, NX):
            t_copy(k, b, d).wait_recv()
        if backward:
            carry = jnp.where(x < NX - 1, tin[k, NX - 1, at, :], 0.0)
            for xs in range(NX - 2, 0, -1):
                carry = jnp.where(x < xs, times(carry, segs[1, xs]) + tin[k, xs, at, :], carry)
        else:
            carry = jnp.where(x > 0, tin[k, 0, at, :], 0.0)
            for xs in range(1, NX - 1):
                carry = jnp.where(x > xs, times(carry, segs[0, xs]) + tin[k, xs, at, :], carry)
        for n in range(NZ):
            if n == edge:
                eout[k, spot(k, b, n), :] = carry
            else:
                tile = maps[carry_kind, n + (1 if backward else 0)]
                eout[k, spot(k, b, n), :] = eout[k, spot(k, b, n), :] + times(carry, tile)
        for d in far_first:
            e_copy(k, b, d).start()
        ein[k, spot(k, b, z), :] = eout[k, spot(k, b, z), :]

    def arrive(k, b):
        for d in far_first[::-1]:
            e_copy(k, b, d).wait_recv()

    def relax(k, b, ahead, old):
        first, last = EDGES[k][b], EDGES[k][b + 1]
        lo = 0 if b == 0 else first + ahead
        hi = SIDE if b == BANDS - 1 else last + ahead
        for p, q in split(lo, hi):
            value = start[px(p, q), :] + STEP * conv(x3a, p, q, w[0])
            mid[px(p, q), :] = value
            fill(x3b, p, q, jnp.tanh(value))
        for p, q in split(first, last):
            value = mid[px(p, q), :] + STEP * conv(x3b, p, q, w[1])
            prop[px(p, q), :] = value
            resout[k, px(p, q), :] = value - old[px(p, q), :]
        send_residual(k, b)


    relax(0, 0, 1, feat)

    def g_pass(d):
        g_copy(d).wait_recv()
        g_forward(d).start()

    each(NZ, g_pass, 1)
    for b in range(1, BANDS):
        relax(0, b, 1, feat)

    each(NZ, lambda d: g_forward(d).wait_recv(), 1)
    made, tiles = {}, {}

    def product(i, j):
        if (i, j) not in made:
            if i == j:
                value = gin[i]
            else:
                step = 1
                while (j // (2 * step)) * 2 * step > i:
                    step *= 2
                m = j // step * step
                value = times(product(i, m - 1), tile_of(m, j))
            made[i, j] = value
        return made[i, j]

    def tile_of(i, j):
        if (i, j) not in tiles:
            value = product(i, j)
            if i == j:
                put(maps, (0, i), value)
                tiles[i, j] = maps.at[0, i]
            elif j == NZ - 1:
                put(maps, (4, i), value)
                tiles[i, j] = maps.at[4, i]
            else:
                n = sum(i2 != j2 and j2 != NZ - 1 for i2, j2 in tiles)
                put(temps, (n,), value)
                tiles[i, j] = temps.at[n]
        return tiles[i, j][...]

    for n in range(NZ):
        tile_of(n, n)
    put(maps, (4, NZ), eye)
    put(maps, (4, NZ - 1), gin[NZ - 1])
    for n in range(NZ - 1):
        tile_of(n, NZ - 1)
    for n in range(NZ):
        prods[1, n] = product(n, NZ - 1)
        prods[0, n + 1] = product(0, n)
        put(maps, (2, n + 1), product(0, n))
    pin[x] = product(0, NZ - 1)

    def p_copy(d):
        return remote(pin.at[x], pin.at[x], p_s.at[d], p_r.at[d], to_x(d))

    each(NX, lambda d: p_copy(d).start(), 1)

    def segments_arrive():
        each(NX, lambda d: p_copy(d).wait_recv(), 1)
        for xs in range(1, NX - 1):
            put(segs, (0, xs), pin[xs])

    for b in range(BANDS):
        scan(0, b, False)

    def turn_kernels(layer):
        def turn(t):
            block = w[layer, pl.ds(pl.multiple_of((8 - t) * CH, CH), CH), :].astype(F32)
            wt[layer, pl.ds(pl.multiple_of(t * CH, CH), CH), :] = block.T.astype(BF16)
        each(9, turn)

    turn_kernels(1)
    turn_kernels(0)

    for b in range(BANDS):
        arrive(0, b)
        for p, q in split(EDGES[0][b], EDGES[0][b + 1]):
            e = ein[0, px(p, q), :]
            ends[px(p, q), :] = prop[px(p, q), :] + times(e, maps[0, z])
            value = start[px(p, q), :] + e
            start[px(p, q), :] = value
            fill(x3a, p, q, jnp.tanh(value))
        relax(1, b, 1, ends)

    loads[3].wait()
    for p, q in split(0, SIDE):
        fill(z3a, p, q, cot[px(p, q), :])
    for p, q in split(0, SIDE):
        ycot[px(p, q), :] = conv(z3a, p, q, wt[1])

    for b in range(BANDS):
        scan(1, b, False)

    def turn_maps(s):
        put(maps, (3, s + 1), prods[0, s + 1].T)

    put(maps, (3, 0), eye)
    each(NZ - 1, turn_maps)

    def pull(k, b, old):
        first, last = EDGES[k][b], EDGES[k][b + 1]
        for p, q in split(first, last):
            value = mid[px(p, q), :] + d0[px(p, q), :] * conv(z3b, p, q, wt[0])
            prop[px(p, q), :] = value
            resout[k, px(p, q), :] = value - old[px(p, q), :]
        send_residual(k, b)

    def behind(k, b):
        lo = 0 if b == 0 else EDGES[k][b] + 1
        hi = SIDE if b == BANDS - 1 else EDGES[k][b + 1] + 1
        return split(lo, hi)

    for b in range(BANDS):
        arrive(1, b)
        for p, q in split(EDGES[1][b], EDGES[1][b + 1]):
            e = ein[1, px(p, q), :]
            ends[px(p, q), :] = prop[px(p, q), :] + times(e, maps[0, z])
            value = start[px(p, q), :] + e
            start[px(p, q), :] = value
            active = jnp.tanh(value)
            d0[px(p, q), :] = STEP * (1.0 - active * active)
            fill(x3a, p, q, active)
        for p, q in behind(2, b):
            active = jnp.tanh(start[px(p, q), :] + STEP * conv(x3a, p, q, w[0]))
            slope = STEP * (1.0 - active * active)
            d1[px(p, q), :] = slope
            fill(x3b, p, q, active)
            value = cot[px(p, q), :] + slope * ycot[px(p, q), :]
            mid[px(p, q), :] = value
            fill(z3b, p, q, value)
        pull(2, b, cot)

    def turn_more_maps(s):
        put(maps, (1, s), gin[s].T)
        put(maps, (5, s), prods[1, s].T)

    each(NZ, turn_more_maps)
    for xs in range(1, NX - 1):
        put(segs, (1, xs), pin[xs].T)

    for b in range(BANDS):
        scan(2, b, True)

    for b in range(BANDS):
        arrive(2, b)
        for p, q in split(EDGES[2][b], EDGES[2][b + 1]):
            f = ein[2, px(p, q), :]
            adj[px(p, q), :] = prop[px(p, q), :] + times(f, maps[1, z])
            value = cot[px(p, q), :] + f
            start[px(p, q), :] = value
            fill(z3a, p, q, value)
        for p, q in behind(3, b):
            value = start[px(p, q), :] + d1[px(p, q), :] * conv(z3a, p, q, wt[1])
            mid[px(p, q), :] = value
            fill(z3b, p, q, value)
        pull(3, b, adj)

    for b in range(BANDS):
        scan(3, b, True)

    def place(core, yy):
        return pl.ds(pl.multiple_of(core * half + yy * part, part), part)

    other = pl.ds(pl.multiple_of((NC - 1 - c) * half, half), half)

    def sib_copy(layer):
        return remote(local_grad.at[layer, other], gs.at[layer], sib_s.at[layer], sib_r.at[layer], to_core())

    def rs_copy(layer, d):
        return remote(hsum.at[layer, lax.rem(y + d, NY)], yin.at[layer, d], rs_s.at[layer, d], rs_r.at[layer, d], to_y(d))

    def ag_copy(layer, d):
        at = place(c, y)
        return remote(grad.at[layer, at], grad.at[layer, at], ag_s.at[layer, d], ag_r.at[layer, d], to_y(d))

    def fw_copy(layer, d):
        at = place(c, lax.rem(y + NY - d, NY))
        return remote(grad.at[layer, at], grad.at[layer, at], fw_s.at[layer, d], fw_r.at[layer, d], to_core())

    def reduce_core(layer):
        sib_copy(layer).wait()
        for yy in range(NY):
            hsum[layer, yy] = local_grad[layer, place(c, yy), :] + gs[layer, pl.ds(yy * part, part), :]
        each(NY, lambda d: rs_copy(layer, d).start(), 1)

    def reduce_chips(layer):
        total = hsum[layer, y]
        for d in range(1, NY):
            rs_copy(layer, d).wait_recv()
            total = total + yin[layer, d]
        grad[layer, place(c, y), :] = total * factor
        each(NY, lambda d: ag_copy(layer, d).start(), 1)
        fw_copy(layer, 0).start()

    def spread(layer):
        def go(d):
            ag_copy(layer, d).wait_recv()
            fw_copy(layer, d).start()
        each(NY, go, 1)

    def gradient(layer, signal, buffer, first, last, more):
        for r in range(3):
            block = jnp.dot(signal[:, px(first, last)], buffer[px(first + r, last + r), :], preferred_element_type=F32)
            for s in range(3):
                t = 3 * r + s
                value = block[:, CH * s : CH * (s + 1)].T
                at = slice(CH * t, CH * (t + 1))
                local_grad[layer, at, :] = local_grad[layer, at, :] + value if more else value

    def adjoint_out(b):
        for p, q in split(EDGES[3][b], EDGES[3][b + 1]):
            adj[px(p, q), :] = prop[px(p, q), :] + times(ein[3, px(p, q), :], maps[1, z])

    def top_signal(p, q):
        value = start[px(p, q), :] + ein[3, px(p, q), :]
        start[px(p, q), :] = value
        fill(z3a, p, q, value)
        zt[:, px(p, q)] = value.T.astype(BF16)

    def lower_signal(p, q):
        value = start[px(p, q), :] + d1[px(p, q), :] * conv(z3a, p, q, wt[1])
        zt0[:, px(p, q)] = value.T.astype(BF16)

    cut = EDGES[3][1] // 4 * 4
    low = (EDGES[3][1] - 1) // 4 * 4
    arrive(3, 0)
    for p, q in split(0, cut, 8):
        top_signal(p, q)
    gradient(1, zt, x3b, 0, cut, False)
    for p, q in ((0, low // 8 * 4), (low // 8 * 4, low)):
        lower_signal(p, q)
    gradient(0, zt0, x3a, 0, low, False)
    adjoint_out(0)
    arrive(3, 1)
    for p, q in split(cut, SIDE, 8):
        top_signal(p, q)
    gradient(1, zt, x3b, cut, SIDE, True)
    sib_copy(1).start()
    for p, q in ((low, (low + SIDE) // 8 * 4), ((low + SIDE) // 8 * 4, SIDE)):
        lower_signal(p, q)
    gradient(0, zt0, x3a, low, SIDE, True)
    sib_copy(0).start()
    reduce_core(1)
    reduce_core(0)
    adjoint_out(1)
    reduce_chips(1)
    spread(1)
    reduce_chips(0)
    spread(0)
    for layer in range(2):
        each(NY, lambda d: fw_copy(layer, d).wait_recv(), 0)

    for layer in range(2):
        each(NY, lambda d: rs_copy(layer, d).wait_send(), 1)
        each(NY, lambda d: ag_copy(layer, d).wait_send(), 1)
        each(NY, lambda d: fw_copy(layer, d).wait_send(), 0)
    each(NZ, lambda d: g_copy(d).wait_send(), 1)
    each(NZ, lambda d: g_forward(d).wait_send(), 1)
    each(NX, lambda d: p_copy(d).wait_send(), 1)
    for k in range(4):
        for b in range(BANDS):
            each(NZ, lambda d: res_copy(k, b, d).wait_send(), 1)
            each(NZ, lambda d: e_copy(k, b, d).wait_send(), 1)
            each(NX, lambda d: t_copy(k, b, d).wait_send(), 1)


def make_local(NX, NZ, NY, NC):
    half = TAPS // NC
    part = half // NY
    dma = pltpu.SemaphoreType.DMA
    vmem = pltpu.VMEM
    image = vmem((PIXELS, CH), F32)
    padded = vmem((PIXELS + 2 * SIDE, 3 * CH), BF16)
    sweeps = vmem((4, PIXELS, CH), F32)
    moves = dma((4 * BANDS, NZ))

    def local(features, cotangent, weights, coarse_map):
        factor = STEP / (features.shape[0] * NY * NC)
        out = pl.pallas_call(
            functools.partial(body, NX, NZ, NY, NC, factor),
            out_shape=(
                jax.ShapeDtypeStruct((PIXELS, CH), F32),
                jax.ShapeDtypeStruct((PIXELS, CH), F32),
                jax.ShapeDtypeStruct((2, TAPS, CH), F32),
            ),
            in_specs=[pl.BlockSpec(memory_space=pl.ANY)] * 4,
            out_specs=[pl.BlockSpec(memory_space=vmem)] * 3,
            scratch_shapes=[
                image, image, vmem((2, TAPS, CH), BF16), vmem((CH, CH), F32),
                padded, padded, padded, padded,
                vmem((2, TAPS, CH), BF16),
                image, image, image, image, image, image,
                vmem((CH, PIXELS), BF16), vmem((CH, PIXELS), BF16),
                sweeps, sweeps, sweeps, sweeps,
                vmem((4, NX, PIXELS // NZ, CH), F32),
                vmem((NZ, CH, CH), F32),
                vmem((NX, CH, CH), F32),
                vmem((2, NZ + 1, CH, CH), F32),
                vmem((NZ, 2 * CH, 2 * CH), BF16),
                vmem((6, NZ + 1, 2 * CH, 2 * CH), BF16),
                vmem((2, NX, 2 * CH, 2 * CH), BF16),
                vmem((2, TAPS, CH), F32),
                vmem((2, half, CH), F32),
                vmem((2, NY, part, CH), F32),
                vmem((2, NY, part, CH), F32),
                dma((4,)),
                moves, moves, moves, moves, dma((4 * BANDS, NX)), dma((4 * BANDS, NX)),
                dma((NZ,)), dma((NZ,)), dma((NZ,)), dma((NZ,)), dma((NX,)), dma((NX,)),
                dma((2,)), dma((2,)), dma((2, NY)), dma((2, NY)), dma((2, NY)), dma((2, NY)), dma((2, NY)), dma((2, NY)),
            ],
            compiler_params=pltpu.CompilerParams(
                collective_id=0, has_side_effects=True, vmem_limit_bytes=56 * 1024 * 1024
            ),
            cost_estimate=pl.CostEstimate(flops=5 * 10**9, bytes_accessed=5 * 10**6, transcendentals=10**6),
        )(
            features.reshape(PIXELS, CH),
            cotangent.reshape(PIXELS, CH),
            weights.reshape(2, TAPS, CH),
            coarse_map.reshape(CH, CH),
        )
        shape = (1, 1, SIDE, SIDE, CH)
        return out[0].reshape(shape), out[1].reshape(shape), out[2].reshape(2, 9, CH, CH)

    return local


def build(mesh, sizes):
    return jax.shard_map(
        make_local(*sizes),
        mesh=mesh,
        in_specs=(P("dp", None, None, None), P("dp", None, None, None), P("tm", None, None, None), P("tm", None, None)),
        out_specs=(P("tm", "dp", None, None, None), P("tm", "dp", None, None, None), P("tm", None, None, None)),
        check_vma=False,
    )


def solution(mesh):
    return build(mesh, (4, 8, 4, 2))
```

time: 1230 us -> 152 us (0.12); the launches traced: 1220 us -> 152 us
  waiting for transfers between devices: 741 us -> 0 us
  matrix products: 222 us -> 0 us
  other arithmetic: 187 us -> 0 us
  Pallas kernels: 0 us -> 146 us
  local copies, waits for them, and re-layouts: 32 us -> 4.85 us
  between operations: 15.4 us -> 0.65 us
    all_gather x6 -> x0, waiting for transfers between devices: 608 us -> none  [carried_in(): everything = jax.tree.map(lambda part: lax.all_gather(part, axis), shard)]
    dot_general x240 -> x0, matrix products: 222 us -> none  [the longest x132 197 us: apply_map(): jnp.dot(vector.reshape(-1, vector.shape[-1]), matrix, precision=lax.Preci...]
    select_n x128 -> x0, other arithmetic: 169 us -> none  [turn(): return jax.tree.map(lambda a, b: jnp.where(reached, a, b), new, before)]
    pallas_call x0 -> x1, Pallas kernels: none -> 146 us  [local(): pl.pallas_call(functools.partial(body, NX, NZ, NY, NC, factor), out_shape...]
    ppermute x6 -> x0, waiting for transfers between devices: 66.7 us -> none  [from_behind(): return lax.ppermute(shard, axis, pairs)]
    psum x1 -> x0, waiting for transfers between devices: 65.7 us -> none  [local(): stacked = lax.psum(stacked, 'dp') * factor]
    dot_general x128 -> x0, local copies, waits for them, and re-layouts: 24.3 us -> none  [apply_map(): jnp.dot(vector.reshape(-1, vector.shape[-1]), matrix, precision=lax.Preci...]
  transfers between devices with their start and end apart: 13 -> 0, of which waited for: 12 -> 0; matrix products, arithmetic and copies ran while one was open for 10% -> 0% of each run, Pallas kernels for 0% -> 0%
where the time goes in v1:
time: 152 us
  Pallas kernels  146 us (96%)
  local copies, waits for them, and re-layouts  4.85 us (3%)
    pallas_call x1, Pallas kernels, local(): pl.pallas_call(functools.partial(body, NX, NZ, NY, NC, factor), out_shape...  146 us
    unnamed x5, local copies, waits for them, and re-layouts  4.85 us

profile of v1, /device:TPU:1, one launch (start us, length us, event | category | flops | bytes accessed | tf_op | source)
XLA Modules:
  0.0 151.6 jit_solution(2765158207207868375)
XLA Ops:
  0.6 146.1 %shard_map.67 = (f32[1024,128]{1,0:T(8,128)}, f32[1024,128]{1,0:T(8,128)}, f32[2,1152,128]{2,1,0:T(8,128)}) custom-call(f32[1024,128]{1,0:T(8,128)} %bitcast.11, f32[1024,128]{1,0:T(8,128)} %bitcast.12, bf16[2,1152,128]{2,1,0:T(8,128)(2,1)} %bitcast.10, f32[128,128]{1,0:T(8,128)} %bitcast.13), custom_call_target="tpu_custom_call" | custom-call | flops 5000000000 | bytes 5000000 | tf_op jit(solution)/shard_map/pallas_call | solution.py:533
  146.8 0.0 copy-start
  146.8 2.0 %copy.10 = f32[1,1,32,32,128]{4,3,2,1,0:T(8,128)} copy(f32[1,1,32,32,128]{4,3,2,1,0:T(8,128)} %bitcast.9) | data formatting | bytes 1048576
  148.8 1.9 %copy.11 = f32[1,1,32,32,128]{4,3,2,1,0:T(8,128)} copy(f32[1,1,32,32,128]{4,3,2,1,0:T(8,128)} %bitcast.8) | data formatting | bytes 1048576
  150.6 0.0 copy-done
  150.6 1.0 copy.12
Async XLA Ops:
  146.8 3.8 %copy-start = (f32[2,1152,128]{2,1,0:T(8,128)S(1)}, f32[2,1152,128]{2,1,0:T(8,128)}, u32[]{:S(2)}) copy-start(f32[2,1152,128]{2,1,0:T(8,128)} %get-tuple-element.8) | copy-start | bytes 3538948

commit v2 on v1

--- a/solution.py
+++ b/solution.py
@@ -44,6 +44,7 @@
     x3a, x3b, z3a, z3b, wt, start, mid, prop, d0, d1, ycot, zt, zt0,
     resout, resin, eout, ein, tin, gin, pin, prods, temps, maps, segs, local_grad, gs, hsum, yin,
     in_s,
+    relay, hop_s, hop_r, land_s, land_r,
     res_s, res_r, e_s, e_r, t_s, t_r, g_s, g_r, gf_s, gf_r, p_s, p_r, sib_s, sib_r, rs_s, rs_r, ag_s, ag_r, fw_s, fw_r,
 ):
     loads = [
@@ -58,7 +59,8 @@
     y, c = dp // NC, lax.rem(dp, NC)
     half = TAPS // NC
     part = half // NY
-    far_first = sorted(range(1, NZ), key=lambda d: -min(d, NZ - d))
+    opposite = NZ // 2 if NZ > 2 else 0
+    far_first = sorted((d for d in range(1, NZ) if d != opposite), key=lambda d: -min(d, NZ - d))
 
     def to_z(d):
         return {"tm": x * NZ + lax.rem(z + d, NZ)}
@@ -135,7 +137,7 @@
         zs = lax.rem(z + NZ - d, NZ)
         return remote(gin.at[zs, gh], gin.at[zs, gh], gf_s.at[d], gf_r.at[d], to_core())
 
-    for d in far_first:
+    for d in sorted(range(1, NZ), key=lambda d: -min(d, NZ - d)):
         g_copy(d).start()
 
     def share(k, b):
@@ -156,6 +158,7 @@
         )
 
     def send_residual(k, b):
+        hop(0, k, b)
         for d in far_first:
             res_copy(k, b, d).start()
         resin[k, spot(k, b, z), :] = resout[k, spot(k, b, z), :]
@@ -173,6 +176,47 @@
         zp = lax.rem(z + d, NZ)
         m = BANDS * k + b
         return remote(eout.at[k, spot(k, b, zp)], ein.at[k, spot(k, b, z)], e_s.at[m, d], e_r.at[m, d], to_z(d))
+
+    def piece(k, b, n, side):
+        base, R = share(k, b)
+        cut = R // 16 * 8
+        size = R - cut if side else cut
+        return pl.ds(pl.multiple_of(base + n * R + (cut if side else 0), 8), size), size
+
+    def ends_of(way):
+        return (resout, resin) if way == 0 else (eout, ein)
+
+    def hop_copy(way, k, b, side):
+        m = BANDS * k + b
+        at, size = piece(k, b, lax.rem(z + opposite, NZ), side)
+        return remote(
+            ends_of(way)[0].at[k, at], relay.at[way, m, side, :size],
+            hop_s.at[way, m, side], hop_r.at[way, m, side], to_z(NZ - 1 if side else 1),
+        )
+
+    def land_copy(way, k, b, side):
+        m = BANDS * k + b
+        at, size = piece(k, b, lax.rem(z + (1 if side else NZ - 1), NZ), side)
+        return remote(
+            relay.at[way, m, side, :size], ends_of(way)[1].at[k, at],
+            land_s.at[way, m, side], land_r.at[way, m, side], to_z(NZ - opposite + 1 if side else opposite - 1),
+        )
+
+    def hop(way, k, b):
+        if opposite:
+            for side in range(2):
+                hop_copy(way, k, b, side).start()
+
+    def pass_on(way, k, b):
+        if opposite:
+            for side in range(2):
+                hop_copy(way, k, b, side).wait_recv()
+                land_copy(way, k, b, side).start()
+
+    def landed(way, k, b):
+        if opposite:
+            for side in range(2):
+                land_copy(way, k, b, side).wait_recv()
 
     def put(where, index, matrix):
         high, low = two_terms(matrix)
@@ -187,6 +231,7 @@
         edge = NZ - 1 if backward else 0
         for d in far_first[::-1]:
             res_copy(k, b, d).wait_recv()
+        landed(0, k, b)
         inner = NZ - 1 - edge
         total = resin[k, spot(k, b, inner), :]
         for s in range(NZ):
@@ -195,6 +240,10 @@
         tin[k, x, at, :] = total
         for d in range(1, NX):
             t_copy(k, b, d).start()
+        if b == 0:
+            pass_on(0, k, 1)
+        else:
+            pass_on(1, k, 0)
         run = {}
         if backward:
             value = resin[k, spot(k, b, NZ - 1), :]
@@ -228,6 +277,7 @@
             else:
                 tile = maps[carry_kind, n + (1 if backward else 0)]
                 eout[k, spot(k, b, n), :] = eout[k, spot(k, b, n), :] + times(carry, tile)
+        hop(1, k, b)
         for d in far_first:
             e_copy(k, b, d).start()
         ein[k, spot(k, b, z), :] = eout[k, spot(k, b, z), :]
@@ -235,6 +285,7 @@
     def arrive(k, b):
         for d in far_first[::-1]:
             e_copy(k, b, d).wait_recv()
+        landed(1, k, b)
 
     def relax(k, b, ahead, old):
         first, last = EDGES[k][b], EDGES[k][b + 1]
@@ -248,7 +299,11 @@
             value = mid[px(p, q), :] + STEP * conv(x3b, p, q, w[1])
             prop[px(p, q), :] = value
             resout[k, px(p, q), :] = value - old[px(p, q), :]
+        if b == 0 and k > 0:
+            pass_on(1, k - 1, 1)
         send_residual(k, b)
+        if b == 1:
+            pass_on(0, k, 0)
 
 
     relax(0, 0, 1, feat)
@@ -357,7 +412,11 @@
             value = mid[px(p, q), :] + d0[px(p, q), :] * conv(z3b, p, q, wt[0])
             prop[px(p, q), :] = value
             resout[k, px(p, q), :] = value - old[px(p, q), :]
+        if b == 0 and k > 0:
+            pass_on(1, k - 1, 1)
         send_residual(k, b)
+        if b == 1:
+            pass_on(0, k, 0)
 
     def behind(k, b):
         lo = 0 if b == 0 else EDGES[k][b] + 1
@@ -478,6 +537,7 @@
     cut = EDGES[3][1] // 4 * 4
     low = (EDGES[3][1] - 1) // 4 * 4
     arrive(3, 0)
+    pass_on(1, 3, 1)
     for p, q in split(0, cut, 8):
         top_signal(p, q)
     gradient(1, zt, x3b, 0, cut, False)
@@ -513,8 +573,14 @@
     each(NX, lambda d: p_copy(d).wait_send(), 1)
     for k in range(4):
         for b in range(BANDS):
-            each(NZ, lambda d: res_copy(k, b, d).wait_send(), 1)
-            each(NZ, lambda d: e_copy(k, b, d).wait_send(), 1)
+            for d in far_first:
+                res_copy(k, b, d).wait_send()
+                e_copy(k, b, d).wait_send()
+            if opposite:
+                for way in range(2):
+                    for side in range(2):
+                        hop_copy(way, k, b, side).wait_send()
+                        land_copy(way, k, b, side).wait_send()
             each(NX, lambda d: t_copy(k, b, d).wait_send(), 1)
 
 
@@ -558,12 +624,14 @@
                 vmem((2, NY, part, CH), F32),
                 vmem((2, NY, part, CH), F32),
                 dma((4,)),
+                vmem((2, 4 * BANDS, 2, 48 * 8 // NZ, CH), F32),
+                dma((2, 4 * BANDS, 2)), dma((2, 4 * BANDS, 2)), dma((2, 4 * BANDS, 2)), dma((2, 4 * BANDS, 2)),
                 moves, moves, moves, moves, dma((4 * BANDS, NX)), dma((4 * BANDS, NX)),
                 dma((NZ,)), dma((NZ,)), dma((NZ,)), dma((NZ,)), dma((NX,)), dma((NX,)),
                 dma((2,)), dma((2,)), dma((2, NY)), dma((2, NY)), dma((2, NY)), dma((2, NY)), dma((2, NY)), dma((2, NY)),
             ],
             compiler_params=pltpu.CompilerParams(
-                collective_id=0, has_side_effects=True, vmem_limit_bytes=56 * 1024 * 1024
+                collective_id=0, has_side_effects=True, vmem_limit_bytes=40 * 1024 * 1024
             ),
             cost_estimate=pl.CostEstimate(flops=5 * 10**9, bytes_accessed=5 * 10**6, transcendentals=10**6),
         )(

time: 152 us -> 172 us (1.13)
  Pallas kernels: 146 us -> 164 us
  local copies, waits for them, and re-layouts: 4.85 us -> 6.58 us
    pallas_call x1, Pallas kernels: 146 us -> 164 us  [local(): pl.pallas_call(functools.partial(body, NX, NZ, NY, NC, factor), out_shape...]
    unnamed x5 -> x11, local copies, waits for them, and re-layouts: 4.85 us -> 6.58 us
where the time goes in v2:
time: 172 us; the launch traced here: 171 us
  Pallas kernels  164 us (95%)
  local copies, waits for them, and re-layouts  6.58 us (4%)
    pallas_call x1, Pallas kernels, local(): pl.pallas_call(functools.partial(body, NX, NZ, NY, NC, factor), out_shape...  164 us
    unnamed x11, local copies, waits for them, and re-layouts  6.58 us

profile of v2, /device:TPU:1, one launch (start us, length us, event | category | flops | bytes accessed | tf_op | source)
XLA Modules:
  0.0 171.2 jit_solution(15359601496787165077)
XLA Ops:
  0.6 0.0 copy-start
  0.6 1.1 copy-done
  1.7 0.0 copy-start.1
  1.7 1.0 copy-done.1
  2.7 0.0 copy-start.2
  2.7 1.0 copy-done.2
  3.8 0.0 copy-start.3
  3.8 0.8 copy-done.3
  4.6 164.0 %shard_map.67 = (f32[1024,128]{1,0:T(8,128)S(1)}, f32[1024,128]{1,0:T(8,128)S(1)}, f32[2,1152,128]{2,1,0:T(8,128)S(1)}) custom-call(f32[1024,128]{1,0:T(8,128)S(1)} %bitcast.11, f32[1024,128]{1,0:T(8,128)S(1)} %bitcast.12, bf16[2,1152,128]{2,1,0:T(8,128)(2,1)S(1)} %bitcast.10, f32[128,128]{1,0:T(8,128)S(1)} %bitcast.13), custom_call_target="tpu_custom_call" | custom-call | flops 5000000000 | bytes 5000000 | tf_op jit(solution)/shard_map/pallas_call | solution.py:599
  168.6 0.8 copy.10
  169.4 0.8 copy.11
  170.2 1.0 copy.12
Async XLA Ops:
  0.6 1.1 copy-start
  1.7 1.0 copy-start.1
  2.7 1.0 copy-start.2
  3.8 0.8 copy-start.3

commit v3 on v1

--- a/solution.py
+++ b/solution.py
@@ -14,7 +14,7 @@
 PIXELS = SIDE * SIDE
 CH = 128
 BANDS = 2
-EDGES = ((0, 22, 32), (0, 20, 32), (0, 18, 32), (0, 16, 32))
+EDGES = ((0, 20, 32), (0, 18, 32), (0, 16, 32), (0, 14, 32))
 TAPS = 9 * CH
 F32, BF16 = jnp.float32, jnp.bfloat16
 
@@ -181,17 +181,32 @@
         where[(*index, slice(CH, None), slice(0, CH))] = high
         where[(*index, slice(CH, None), slice(CH, None))] = jnp.zeros((CH, CH), BF16)
 
-    def scan(k, b, backward):
+    def sent(k, b):
+        for d in far_first:
+            res_copy(k, b, d).wait_send()
+            e_copy(k, b, d).wait_send()
+        for d in range(1, NX):
+            t_copy(k, b, d).wait_send()
+
+    def scan(k, b, backward, meanwhile=None):
         total_kind, chain_kind, carry_kind = (3, 1, 5) if backward else (4, 0, 2)
         at = t_spot(k, b)
         edge = NZ - 1 if backward else 0
-        for d in far_first[::-1]:
+
+        def term(d):
+            s = lax.rem(z + NZ - d, NZ)
+            return times(resin[k, spot(k, b, s), :], maps[total_kind, s + (0 if backward else 1)])
+
+        near = far_first[::-1][: NZ // 2]
+        for d in near:
             res_copy(k, b, d).wait_recv()
-        inner = NZ - 1 - edge
-        total = resin[k, spot(k, b, inner), :]
-        for s in range(NZ):
-            if s != inner:
-                total = total + times(resin[k, spot(k, b, s), :], maps[total_kind, s + (0 if backward else 1)])
+        total = term(0)
+        for d in near:
+            total = total + term(d)
+        for d in far_first[::-1][NZ // 2 :]:
+            res_copy(k, b, d).wait_recv()
+        for d in far_first[::-1][NZ // 2 :]:
+            total = total + term(d)
         tin[k, x, at, :] = total
         for d in range(1, NX):
             t_copy(k, b, d).start()
@@ -210,8 +225,10 @@
                 run[s + 1] = value
         for n in run:
             eout[k, spot(k, b, n), :] = run[n]
-        if (k, b) == (0, 0):
-            segments_arrive()
+        if meanwhile is not None:
+            meanwhile()
+        if k > 0:
+            sent(k - 1, b)
         for d in range(1, NX):
             t_copy(k, b, d).wait_recv()
         if backward:
@@ -314,17 +331,18 @@
         for xs in range(1, NX - 1):
             put(segs, (0, xs), pin[xs])
 
-    for b in range(BANDS):
-        scan(0, b, False)
-
     def turn_kernels(layer):
         def turn(t):
             block = w[layer, pl.ds(pl.multiple_of((8 - t) * CH, CH), CH), :].astype(F32)
             wt[layer, pl.ds(pl.multiple_of(t * CH, CH), CH), :] = block.T.astype(BF16)
         each(9, turn)
 
-    turn_kernels(1)
-    turn_kernels(0)
+    def first_slot():
+        segments_arrive()
+        turn_kernels(1)
+
+    for b in range(BANDS):
+        scan(0, b, False, (first_slot, lambda: turn_kernels(0), None)[b])
 
     for b in range(BANDS):
         arrive(0, b)
@@ -336,20 +354,22 @@
             fill(x3a, p, q, jnp.tanh(value))
         relax(1, b, 1, ends)
 
-    loads[3].wait()
-    for p, q in split(0, SIDE):
-        fill(z3a, p, q, cot[px(p, q), :])
-    for p, q in split(0, SIDE):
-        ycot[px(p, q), :] = conv(z3a, p, q, wt[1])
-
-    for b in range(BANDS):
-        scan(1, b, False)
-
     def turn_maps(s):
         put(maps, (3, s + 1), prods[0, s + 1].T)
 
-    put(maps, (3, 0), eye)
-    each(NZ - 1, turn_maps)
+    def second_slot():
+        put(maps, (3, 0), eye)
+        each(NZ - 1, turn_maps)
+
+    def third_slot():
+        loads[3].wait()
+        for p, q in split(0, SIDE):
+            fill(z3a, p, q, cot[px(p, q), :])
+        for p, q in split(0, SIDE):
+            ycot[px(p, q), :] = conv(z3a, p, q, wt[1])
+
+    for b in range(BANDS):
+        scan(1, b, False, (second_slot, third_slot, None)[b])
 
     def pull(k, b, old):
         first, last = EDGES[k][b], EDGES[k][b + 1]
@@ -384,16 +404,23 @@
             fill(z3b, p, q, value)
         pull(2, b, cot)
 
-    def turn_more_maps(s):
+    def turn_steps(s):
         put(maps, (1, s), gin[s].T)
+
+    def turn_carries(s):
         put(maps, (5, s), prods[1, s].T)
 
-    each(NZ, turn_more_maps)
-    for xs in range(1, NX - 1):
-        put(segs, (1, xs), pin[xs].T)
-
-    for b in range(BANDS):
-        scan(2, b, True)
+    def fourth_slot():
+        each(NZ, turn_carries)
+        each(NZ, lambda d: g_copy(d).wait_send(), 1)
+        each(NZ, lambda d: g_forward(d).wait_send(), 1)
+        each(NX, lambda d: p_copy(d).wait_send(), 1)
+        for xs in range(1, NX - 1):
+            put(segs, (1, xs), pin[xs].T)
+
+    each(NZ, turn_steps)
+    for b in range(BANDS):
+        scan(2, b, True, (fourth_slot, None, None)[b])
 
     for b in range(BANDS):
         arrive(2, b)
@@ -475,31 +502,35 @@
         value = start[px(p, q), :] + d1[px(p, q), :] * conv(z3a, p, q, wt[1])
         zt0[:, px(p, q)] = value.T.astype(BF16)
 
-    cut = EDGES[3][1] // 4 * 4
-    low = (EDGES[3][1] - 1) // 4 * 4
-    arrive(3, 0)
-    for p, q in split(0, cut, 8):
-        top_signal(p, q)
-    gradient(1, zt, x3b, 0, cut, False)
-    for p, q in ((0, low // 8 * 4), (low // 8 * 4, low)):
-        lower_signal(p, q)
-    gradient(0, zt0, x3a, 0, low, False)
-    adjoint_out(0)
-    arrive(3, 1)
-    for p, q in split(cut, SIDE, 8):
-        top_signal(p, q)
-    gradient(1, zt, x3b, cut, SIDE, True)
-    sib_copy(1).start()
-    for p, q in ((low, (low + SIDE) // 8 * 4), ((low + SIDE) // 8 * 4, SIDE)):
-        lower_signal(p, q)
-    gradient(0, zt0, x3a, low, SIDE, True)
+    cuts = [e // 4 * 4 for e in EDGES[3]]
+    lows = [0] + [(e - 1) // 4 * 4 for e in cuts[1:-1]] + [SIDE]
+
+    def halves(first, last):
+        middle = (first + last) // 8 * 4
+        return [(p, q) for p, q in ((first, middle), (middle, last)) if q > p]
+
+    for b in range(BANDS):
+        arrive(3, b)
+        for p, q in halves(cuts[b], cuts[b + 1]):
+            top_signal(p, q)
+        gradient(1, zt, x3b, cuts[b], cuts[b + 1], b > 0)
+        if b == BANDS - 1:
+            sib_copy(1).start()
+        for p, q in halves(lows[b], lows[b + 1]):
+            lower_signal(p, q)
+        if b == BANDS - 1:
+            reduce_core(1)
+        gradient(0, zt0, x3a, lows[b], lows[b + 1], b > 0)
+        if b < BANDS - 1:
+            adjoint_out(b)
     sib_copy(0).start()
-    reduce_core(1)
+    adjoint_out(BANDS - 1)
     reduce_core(0)
-    adjoint_out(1)
     reduce_chips(1)
+    reduce_chips(0)
+    for b in range(BANDS):
+        sent(3, b)
     spread(1)
-    reduce_chips(0)
     spread(0)
     for layer in range(2):
         each(NY, lambda d: fw_copy(layer, d).wait_recv(), 0)
@@ -508,14 +539,6 @@
         each(NY, lambda d: rs_copy(layer, d).wait_send(), 1)
         each(NY, lambda d: ag_copy(layer, d).wait_send(), 1)
         each(NY, lambda d: fw_copy(layer, d).wait_send(), 0)
-    each(NZ, lambda d: g_copy(d).wait_send(), 1)
-    each(NZ, lambda d: g_forward(d).wait_send(), 1)
-    each(NX, lambda d: p_copy(d).wait_send(), 1)
-    for k in range(4):
-        for b in range(BANDS):
-            each(NZ, lambda d: res_copy(k, b, d).wait_send(), 1)
-            each(NZ, lambda d: e_copy(k, b, d).wait_send(), 1)
-            each(NX, lambda d: t_copy(k, b, d).wait_send(), 1)
 
 
 def make_local(NX, NZ, NY, NC):
@@ -537,7 +560,7 @@
                 jax.ShapeDtypeStruct((PIXELS, CH), F32),
                 jax.ShapeDtypeStruct((2, TAPS, CH), F32),
             ),
-            in_specs=[pl.BlockSpec(memory_space=pl.ANY)] * 4,
+            in_specs=[pl.BlockSpec(memory_space=pltpu.HBM)] * 4,
             out_specs=[pl.BlockSpec(memory_space=vmem)] * 3,
             scratch_shapes=[
                 image, image, vmem((2, TAPS, CH), BF16), vmem((CH, CH), F32),
@@ -563,7 +586,7 @@
                 dma((2,)), dma((2,)), dma((2, NY)), dma((2, NY)), dma((2, NY)), dma((2, NY)), dma((2, NY)), dma((2, NY)),
             ],
             compiler_params=pltpu.CompilerParams(
-                collective_id=0, has_side_effects=True, vmem_limit_bytes=56 * 1024 * 1024
+                collective_id=0, has_side_effects=True, vmem_limit_bytes=48 * 1024 * 1024
             ),
             cost_estimate=pl.CostEstimate(flops=5 * 10**9, bytes_accessed=5 * 10**6, transcendentals=10**6),
         )(

time: 152 us -> 148 us (0.974)
  Pallas kernels: 146 us -> 141 us
  local copies, waits for them, and re-layouts: 4.85 us -> 6.58 us
    pallas_call x1, Pallas kernels: 146 us -> 141 us  [local(): pl.pallas_call(functools.partial(body, NX, NZ, NY, NC, factor), out_shape...]
    unnamed x5 -> x11, local copies, waits for them, and re-layouts: 4.85 us -> 6.58 us
where the time goes in v3:
time: 148 us
  Pallas kernels  141 us (95%)
  local copies, waits for them, and re-layouts  6.58 us (4%)
    pallas_call x1, Pallas kernels, local(): pl.pallas_call(functools.partial(body, NX, NZ, NY, NC, factor), out_shape...  141 us
    unnamed x11, local copies, waits for them, and re-layouts  6.58 us

profile of v3, /device:TPU:1, one launch (start us, length us, event | category | flops | bytes accessed | tf_op | source)
XLA Modules:
  0.0 147.9 jit_solution(9111568069692651532)
XLA Ops:
  0.6 0.0 copy-start
  0.6 1.1 copy-done
  1.7 0.0 copy-start.1
  1.7 1.0 copy-done.1
  2.7 0.0 copy-start.2
  2.7 1.0 copy-done.2
  3.8 0.0 copy-start.3
  3.8 0.8 copy-done.3
  4.6 140.7 %shard_map.67 = (f32[1024,128]{1,0:T(8,128)S(1)}, f32[1024,128]{1,0:T(8,128)S(1)}, f32[2,1152,128]{2,1,0:T(8,128)S(1)}) custom-call(f32[1024,128]{1,0:T(8,128)S(1)} %bitcast.11, f32[1024,128]{1,0:T(8,128)S(1)} %bitcast.12, bf16[2,1152,128]{2,1,0:T(8,128)(2,1)S(1)} %bitcast.10, f32[128,128]{1,0:T(8,128)S(1)} %bitcast.13), custom_call_target="tpu_custom_call" | custom-call | flops 5000000000 | bytes 5000000 | tf_op jit(solution)/shard_map/pallas_call | solution.py:556
  145.3 0.8 copy.10
  146.1 0.8 copy.11
  146.9 1.0 copy.12
Async XLA Ops:
  0.6 1.1 copy-start
  1.7 1.0 copy-start.1
  2.7 1.0 copy-start.2
  3.8 0.8 copy-start.3

commit v4 on v3

--- a/solution.py
+++ b/solution.py
@@ -13,8 +13,8 @@
 SIDE = 32
 PIXELS = SIDE * SIDE
 CH = 128
-BANDS = 2
-EDGES = ((0, 20, 32), (0, 18, 32), (0, 16, 32), (0, 14, 32))
+BANDS = 3
+EDGES = ((0, 14, 24, 32), (0, 12, 22, 32), (0, 10, 20, 32), (0, 8, 18, 32))
 TAPS = 9 * CH
 F32, BF16 = jnp.float32, jnp.bfloat16
 
@@ -586,7 +586,7 @@
                 dma((2,)), dma((2,)), dma((2, NY)), dma((2, NY)), dma((2, NY)), dma((2, NY)), dma((2, NY)), dma((2, NY)),
             ],
             compiler_params=pltpu.CompilerParams(
-                collective_id=0, has_side_effects=True, vmem_limit_bytes=48 * 1024 * 1024
+                collective_id=0, has_side_effects=True, vmem_limit_bytes=56 * 1024 * 1024
             ),
             cost_estimate=pl.CostEstimate(flops=5 * 10**9, bytes_accessed=5 * 10**6, transcendentals=10**6),
         )(

time: 148 us -> 149 us (level)
  Pallas kernels: 141 us -> 143 us
  local copies, waits for them, and re-layouts: 6.58 us -> 4.85 us
    pallas_call x1, Pallas kernels: 141 us -> 143 us  [local(): pl.pallas_call(functools.partial(body, NX, NZ, NY, NC, factor), out_shape...]
    unnamed x11 -> x5, local copies, waits for them, and re-layouts: 6.58 us -> 4.85 us
where the time goes in v4:
time: 149 us
  Pallas kernels  143 us (96%)
  local copies, waits for them, and re-layouts  4.85 us (3%)
    pallas_call x1, Pallas kernels, local(): pl.pallas_call(functools.partial(body, NX, NZ, NY, NC, factor), out_shape...  143 us
    unnamed x5, local copies, waits for them, and re-layouts  4.85 us

profile of v4, /device:TPU:1, one launch (start us, length us, event | category | flops | bytes accessed | tf_op | source)
XLA Modules:
  0.0 148.8 jit_solution(7745836114199252487)
XLA Ops:
  0.6 143.3 %shard_map.67 = (f32[1024,128]{1,0:T(8,128)}, f32[1024,128]{1,0:T(8,128)}, f32[2,1152,128]{2,1,0:T(8,128)}) custom-call(f32[1024,128]{1,0:T(8,128)} %bitcast.11, f32[1024,128]{1,0:T(8,128)} %bitcast.12, bf16[2,1152,128]{2,1,0:T(8,128)(2,1)} %bitcast.10, f32[128,128]{1,0:T(8,128)} %bitcast.13), custom_call_target="tpu_custom_call" | custom-call | flops 5000000000 | bytes 5000000 | tf_op jit(solution)/shard_map/pallas_call | solution.py:556
  143.9 0.0 copy-start
  144.0 2.0 %copy.10 = f32[1,1,32,32,128]{4,3,2,1,0:T(8,128)} copy(f32[1,1,32,32,128]{4,3,2,1,0:T(8,128)} %bitcast.9) | data formatting | bytes 1048576
  145.9 1.9 %copy.11 = f32[1,1,32,32,128]{4,3,2,1,0:T(8,128)} copy(f32[1,1,32,32,128]{4,3,2,1,0:T(8,128)} %bitcast.8) | data formatting | bytes 1048576
  147.8 0.0 copy-done
  147.8 1.0 copy.12
Async XLA Ops:
  143.9 3.8 %copy-start = (f32[2,1152,128]{2,1,0:T(8,128)S(1)}, f32[2,1152,128]{2,1,0:T(8,128)}, u32[]{:S(2)}) copy-start(f32[2,1152,128]{2,1,0:T(8,128)} %get-tuple-element.8) | copy-start | bytes 3538948

commit v5 on v3

--- a/solution.py
+++ b/solution.py
@@ -30,9 +30,9 @@
     return both[:, :CH] + both[:, CH:]
 
 
-def split(first, last, most=10):
+def split(first, last, most=12):
     count = -(-(last - first) // most)
-    cuts = [first + (last - first) * n // count for n in range(count + 1)]
+    cuts = [first + (last - first) * n // (2 * count) * 2 for n in range(count)] + [last]
     return list(zip(cuts[:-1], cuts[1:]))
 
 
@@ -41,7 +41,7 @@
     feat_in, cot_in, w_in, cm_in,
     ends, adj, grad,
     feat, cot, w, cm,
-    x3a, x3b, z3a, z3b, wt, start, mid, prop, d0, d1, ycot, zt, zt0,
+    x3a, x3b, z3a, z3b, wt, ww, wwt, start, mid, prop, d0, d1, ycot, zt, zt0,
     resout, resin, eout, ein, tin, gin, pin, prods, temps, maps, segs, local_grad, gs, hsum, yin,
     in_s,
     res_s, res_r, e_s, e_r, t_s, t_r, g_s, g_r, gf_s, gf_r, p_s, p_r, sib_s, sib_r, rs_s, rs_r, ag_s, ag_r, fw_s, fw_r,
@@ -107,8 +107,22 @@
         buffer[at, 2 * CH :] = right.astype(BF16)
 
     def conv(buffer, first, last, kernel):
-        pieces = [buffer[px(first + r, last + r), :] for r in range(3)]
-        return jnp.dot(jnp.concatenate(pieces, 1), kernel, preferred_element_type=F32)
+        odd = (last - first) % 2
+        top = first - odd if last == SIDE else first
+        pairs = range((last - first + odd) // 2)
+        pieces = [
+            jnp.concatenate([buffer[px(top + 2 * m + r, top + 2 * m + r + 1), :] for m in pairs], 0) for r in range(4)
+        ]
+        both = jnp.dot(jnp.concatenate(pieces, 1), kernel[...], preferred_element_type=F32)
+        rows = [both[px(m, m + 1), CH * h : CH * (h + 1)] for m in pairs for h in range(2)]
+        return jnp.concatenate(rows[first - top : last - top], 0)
+
+    def widen(wide, layer, source):
+        for r in range(4):
+            at = slice(3 * CH * r, 3 * CH * (r + 1))
+            zero = jnp.zeros((3 * CH, CH), BF16)
+            wide[layer, at, :CH] = source[layer, 3 * CH * r : 3 * CH * (r + 1), :] if r < 3 else zero
+            wide[layer, at, CH:] = source[layer, 3 * CH * (r - 1) : 3 * CH * r, :] if r > 0 else zero
 
     zero_row = jnp.zeros((SIDE, 3 * CH), BF16)
     for buffer in (x3a, x3b, z3a, z3b):
@@ -124,6 +138,8 @@
         start[px(p, q), :] = value
         fill(x3a, p, q, jnp.tanh(value))
     loads[2].wait()
+    widen(ww, 0, w)
+    widen(ww, 1, w)
     pl.semaphore_wait(barrier, NZ - 1 + NX - 1 + NY - 1 + 1)
 
     gh = pl.ds(pl.multiple_of(c * (CH // NC), CH // NC), CH // NC)
@@ -231,14 +247,13 @@
             sent(k - 1, b)
         for d in range(1, NX):
             t_copy(k, b, d).wait_recv()
-        if backward:
-            carry = jnp.where(x < NX - 1, tin[k, NX - 1, at, :], 0.0)
-            for xs in range(NX - 2, 0, -1):
-                carry = jnp.where(x < xs, times(carry, segs[1, xs]) + tin[k, xs, at, :], carry)
-        else:
-            carry = jnp.where(x > 0, tin[k, 0, at, :], 0.0)
-            for xs in range(1, NX - 1):
-                carry = jnp.where(x > xs, times(carry, segs[0, xs]) + tin[k, xs, at, :], carry)
+        carry = jnp.zeros((total.shape[0], CH), F32)
+        for lag in range(1, NX):
+            xs = lax.rem(x + (lag if backward else NX - lag), NX)
+            value = tin[k, xs, at, :]
+            if lag > 1:
+                value = times(value, segs[1 if backward else 0, lag])
+            carry = carry + jnp.where(x < NX - lag if backward else x >= lag, value, 0.0)
         for n in range(NZ):
             if n == edge:
                 eout[k, spot(k, b, n), :] = carry
@@ -258,11 +273,11 @@
         lo = 0 if b == 0 else first + ahead
         hi = SIDE if b == BANDS - 1 else last + ahead
         for p, q in split(lo, hi):
-            value = start[px(p, q), :] + STEP * conv(x3a, p, q, w[0])
+            value = start[px(p, q), :] + STEP * conv(x3a, p, q, ww.at[0])
             mid[px(p, q), :] = value
             fill(x3b, p, q, jnp.tanh(value))
         for p, q in split(first, last):
-            value = mid[px(p, q), :] + STEP * conv(x3b, p, q, w[1])
+            value = mid[px(p, q), :] + STEP * conv(x3b, p, q, ww.at[1])
             prop[px(p, q), :] = value
             resout[k, px(p, q), :] = value - old[px(p, q), :]
         send_residual(k, b)
@@ -328,14 +343,26 @@
 
     def segments_arrive():
         each(NX, lambda d: p_copy(d).wait_recv(), 1)
-        for xs in range(1, NX - 1):
-            put(segs, (0, xs), pin[xs])
+        if NX > 2:
+            def segment(lag):
+                return pin[lax.rem(x + NX + lag, NX)]
+
+            back, ahead = segment(-1), segment(1)
+            put(segs, (0, 2), back)
+            prods[2, 2] = ahead
+            for lag in range(3, NX):
+                back = times(segment(1 - lag), segs[0, lag - 1])
+                put(segs, (0, lag), back)
+                put(segs, (1, lag), segment(lag - 1))
+                ahead = times(ahead, segs[1, lag])
+                prods[2, lag] = ahead
 
     def turn_kernels(layer):
         def turn(t):
             block = w[layer, pl.ds(pl.multiple_of((8 - t) * CH, CH), CH), :].astype(F32)
             wt[layer, pl.ds(pl.multiple_of(t * CH, CH), CH), :] = block.T.astype(BF16)
         each(9, turn)
+        widen(wwt, layer, wt)
 
     def first_slot():
         segments_arrive()
@@ -366,7 +393,7 @@
         for p, q in split(0, SIDE):
             fill(z3a, p, q, cot[px(p, q), :])
         for p, q in split(0, SIDE):
-            ycot[px(p, q), :] = conv(z3a, p, q, wt[1])
+            ycot[px(p, q), :] = conv(z3a, p, q, wwt.at[1])
 
     for b in range(BANDS):
         scan(1, b, False, (second_slot, third_slot, None)[b])
@@ -374,7 +401,7 @@
     def pull(k, b, old):
         first, last = EDGES[k][b], EDGES[k][b + 1]
         for p, q in split(first, last):
-            value = mid[px(p, q), :] + d0[px(p, q), :] * conv(z3b, p, q, wt[0])
+            value = mid[px(p, q), :] + d0[px(p, q), :] * conv(z3b, p, q, wwt.at[0])
             prop[px(p, q), :] = value
             resout[k, px(p, q), :] = value - old[px(p, q), :]
         send_residual(k, b)
@@ -395,7 +422,7 @@
             d0[px(p, q), :] = STEP * (1.0 - active * active)
             fill(x3a, p, q, active)
         for p, q in behind(2, b):
-            active = jnp.tanh(start[px(p, q), :] + STEP * conv(x3a, p, q, w[0]))
+            active = jnp.tanh(start[px(p, q), :] + STEP * conv(x3a, p, q, ww.at[0]))
             slope = STEP * (1.0 - active * active)
             d1[px(p, q), :] = slope
             fill(x3b, p, q, active)
@@ -415,8 +442,8 @@
         each(NZ, lambda d: g_copy(d).wait_send(), 1)
         each(NZ, lambda d: g_forward(d).wait_send(), 1)
         each(NX, lambda d: p_copy(d).wait_send(), 1)
-        for xs in range(1, NX - 1):
-            put(segs, (1, xs), pin[xs].T)
+        for lag in range(2, NX):
+            put(segs, (1, lag), prods[2, lag].T)
 
     each(NZ, turn_steps)
     for b in range(BANDS):
@@ -431,7 +458,7 @@
             start[px(p, q), :] = value
             fill(z3a, p, q, value)
         for p, q in behind(3, b):
-            value = start[px(p, q), :] + d1[px(p, q), :] * conv(z3a, p, q, wt[1])
+            value = start[px(p, q), :] + d1[px(p, q), :] * conv(z3a, p, q, wwt.at[1])
             mid[px(p, q), :] = value
             fill(z3b, p, q, value)
         pull(3, b, adj)
@@ -499,7 +526,7 @@
         zt[:, px(p, q)] = value.T.astype(BF16)
 
     def lower_signal(p, q):
-        value = start[px(p, q), :] + d1[px(p, q), :] * conv(z3a, p, q, wt[1])
+        value = start[px(p, q), :] + d1[px(p, q), :] * conv(z3a, p, q, wwt.at[1])
         zt0[:, px(p, q)] = value.T.astype(BF16)
 
     cuts = [e // 4 * 4 for e in EDGES[3]]
@@ -566,13 +593,14 @@
                 image, image, vmem((2, TAPS, CH), BF16), vmem((CH, CH), F32),
                 padded, padded, padded, padded,
                 vmem((2, TAPS, CH), BF16),
+                vmem((2, 12 * CH, 2 * CH), BF16), vmem((2, 12 * CH, 2 * CH), BF16),
                 image, image, image, image, image, image,
                 vmem((CH, PIXELS), BF16), vmem((CH, PIXELS), BF16),
                 sweeps, sweeps, sweeps, sweeps,
                 vmem((4, NX, PIXELS // NZ, CH), F32),
                 vmem((NZ, CH, CH), F32),
                 vmem((NX, CH, CH), F32),
-                vmem((2, NZ + 1, CH, CH), F32),
+                vmem((3, max(NX, NZ + 1), CH, CH), F32),
                 vmem((NZ, 2 * CH, 2 * CH), BF16),
                 vmem((6, NZ + 1, 2 * CH, 2 * CH), BF16),
                 vmem((2, NX, 2 * CH, 2 * CH), BF16),
@@ -586,7 +614,7 @@
                 dma((2,)), dma((2,)), dma((2, NY)), dma((2, NY)), dma((2, NY)), dma((2, NY)), dma((2, NY)), dma((2, NY)),
             ],
             compiler_params=pltpu.CompilerParams(
-                collective_id=0, has_side_effects=True, vmem_limit_bytes=48 * 1024 * 1024
+                collective_id=0, has_side_effects=True, vmem_limit_bytes=56 * 1024 * 1024
             ),
             cost_estimate=pl.CostEstimate(flops=5 * 10**9, bytes_accessed=5 * 10**6, transcendentals=10**6),
         )(

time: 148 us -> 147 us (level)
  local copies, waits for them, and re-layouts: 6.58 us -> 4.85 us
    unnamed x11 -> x5, local copies, waits for them, and re-layouts: 6.58 us -> 4.85 us
where the time goes in v5:
time: 147 us
  Pallas kernels  141 us (96%)
  local copies, waits for them, and re-layouts  4.85 us (3%)
    pallas_call x1, Pallas kernels, local(): pl.pallas_call(functools.partial(body, NX, NZ, NY, NC, factor), out_shape...  141 us
    unnamed x5, local copies, waits for them, and re-layouts  4.85 us

profile of v5, /device:TPU:1, one launch (start us, length us, event | category | flops | bytes accessed | tf_op | source)
XLA Modules:
  0.0 147.0 jit_solution(9559717676648026524)
XLA Ops:
  0.6 141.5 %shard_map.67 = (f32[1024,128]{1,0:T(8,128)}, f32[1024,128]{1,0:T(8,128)}, f32[2,1152,128]{2,1,0:T(8,128)}) custom-call(f32[1024,128]{1,0:T(8,128)} %bitcast.11, f32[1024,128]{1,0:T(8,128)} %bitcast.12, bf16[2,1152,128]{2,1,0:T(8,128)(2,1)} %bitcast.10, f32[128,128]{1,0:T(8,128)} %bitcast.13), custom_call_target="tpu_custom_call" | custom-call | flops 5000000000 | bytes 5000000 | tf_op jit(solution)/shard_map/pallas_call | solution.py:583
  142.1 0.0 copy-start
  142.1 2.0 %copy.10 = f32[1,1,32,32,128]{4,3,2,1,0:T(8,128)} copy(f32[1,1,32,32,128]{4,3,2,1,0:T(8,128)} %bitcast.9) | data formatting | bytes 1048576
  144.1 1.9 %copy.11 = f32[1,1,32,32,128]{4,3,2,1,0:T(8,128)} copy(f32[1,1,32,32,128]{4,3,2,1,0:T(8,128)} %bitcast.8) | data formatting | bytes 1048576
  146.0 0.0 copy-done
  146.0 1.0 copy.12
Async XLA Ops:
  142.1 3.8 %copy-start = (f32[2,1152,128]{2,1,0:T(8,128)S(1)}, f32[2,1152,128]{2,1,0:T(8,128)}, u32[]{:S(2)}) copy-start(f32[2,1152,128]{2,1,0:T(8,128)} %get-tuple-element.8) | copy-start | bytes 3538948

commit v6 on v5

--- a/solution.py
+++ b/solution.py
@@ -59,6 +59,7 @@
     half = TAPS // NC
     part = half // NY
     far_first = sorted(range(1, NZ), key=lambda d: -min(d, NZ - d))
+    sooner, later = far_first[: NZ // 2], far_first[NZ // 2 :]
 
     def to_z(d):
         return {"tm": x * NZ + lax.rem(z + d, NZ)}
@@ -172,7 +173,7 @@
         )
 
     def send_residual(k, b):
-        for d in far_first:
+        for d in far_first if b == 0 else sooner:
             res_copy(k, b, d).start()
         resin[k, spot(k, b, z), :] = resout[k, spot(k, b, z), :]
 
@@ -226,6 +227,11 @@
         tin[k, x, at, :] = total
         for d in range(1, NX):
             t_copy(k, b, d).start()
+        for d in later:
+            if b == 0:
+                res_copy(k, 1, d).start()
+            else:
+                e_copy(k, 0, d).start()
         run = {}
         if backward:
             value = resin[k, spot(k, b, NZ - 1), :]
@@ -260,7 +266,7 @@
             else:
                 tile = maps[carry_kind, n + (1 if backward else 0)]
                 eout[k, spot(k, b, n), :] = eout[k, spot(k, b, n), :] + times(carry, tile)
-        for d in far_first:
+        for d in far_first if b == 1 else sooner:
             e_copy(k, b, d).start()
         ein[k, spot(k, b, z), :] = eout[k, spot(k, b, z), :]
 

time: 147 us -> 148 us (level)
  no operation moved by 1% of the time
where the time goes in v6:
time: 148 us
  Pallas kernels  142 us (96%)
  local copies, waits for them, and re-layouts  4.85 us (3%)
    pallas_call x1, Pallas kernels, local(): pl.pallas_call(functools.partial(body, NX, NZ, NY, NC, factor), out_shape...  142 us
    unnamed x5, local copies, waits for them, and re-layouts  4.85 us

profile of v6, /device:TPU:1, one launch (start us, length us, event | category | flops | bytes accessed | tf_op | source)
XLA Modules:
  0.0 147.9 jit_solution(8152174966456504046)
XLA Ops:
  0.6 142.4 %shard_map.67 = (f32[1024,128]{1,0:T(8,128)}, f32[1024,128]{1,0:T(8,128)}, f32[2,1152,128]{2,1,0:T(8,128)}) custom-call(f32[1024,128]{1,0:T(8,128)} %bitcast.11, f32[1024,128]{1,0:T(8,128)} %bitcast.12, bf16[2,1152,128]{2,1,0:T(8,128)(2,1)} %bitcast.10, f32[128,128]{1,0:T(8,128)} %bitcast.13), custom_call_target="tpu_custom_call" | custom-call | flops 5000000000 | bytes 5000000 | tf_op jit(solution)/shard_map/pallas_call | solution.py:589
  143.0 0.0 copy-start
  143.0 2.0 %copy.10 = f32[1,1,32,32,128]{4,3,2,1,0:T(8,128)} copy(f32[1,1,32,32,128]{4,3,2,1,0:T(8,128)} %bitcast.9) | data formatting | bytes 1048576
  145.0 1.9 %copy.11 = f32[1,1,32,32,128]{4,3,2,1,0:T(8,128)} copy(f32[1,1,32,32,128]{4,3,2,1,0:T(8,128)} %bitcast.8) | data formatting | bytes 1048576
  146.9 0.0 copy-done
  146.9 1.0 copy.12
Async XLA Ops:
  143.0 3.8 %copy-start = (f32[2,1152,128]{2,1,0:T(8,128)S(1)}, f32[2,1152,128]{2,1,0:T(8,128)}, u32[]{:S(2)}) copy-start(f32[2,1152,128]{2,1,0:T(8,128)} %get-tuple-element.8) | copy-start | bytes 3538948

commit v7 on v5

--- a/solution.py
+++ b/solution.py
@@ -58,7 +58,7 @@
     y, c = dp // NC, lax.rem(dp, NC)
     half = TAPS // NC
     part = half // NY
-    far_first = sorted(range(1, NZ), key=lambda d: -min(d, NZ - d))
+    near_first = sorted(range(1, NZ), key=lambda d: min(d, NZ - d))
 
     def to_z(d):
         return {"tm": x * NZ + lax.rem(z + d, NZ)}
@@ -151,7 +151,7 @@
         zs = lax.rem(z + NZ - d, NZ)
         return remote(gin.at[zs, gh], gin.at[zs, gh], gf_s.at[d], gf_r.at[d], to_core())
 
-    for d in far_first:
+    for d in near_first:
         g_copy(d).start()
 
     def share(k, b):
@@ -172,7 +172,7 @@
         )
 
     def send_residual(k, b):
-        for d in far_first:
+        for d in near_first:
             res_copy(k, b, d).start()
         resin[k, spot(k, b, z), :] = resout[k, spot(k, b, z), :]
 
@@ -198,7 +198,7 @@
         where[(*index, slice(CH, None), slice(CH, None))] = jnp.zeros((CH, CH), BF16)
 
     def sent(k, b):
-        for d in far_first:
+        for d in near_first:
             res_copy(k, b, d).wait_send()
             e_copy(k, b, d).wait_send()
         for d in range(1, NX):
@@ -213,15 +213,15 @@
             s = lax.rem(z + NZ - d, NZ)
             return times(resin[k, spot(k, b, s), :], maps[total_kind, s + (0 if backward else 1)])
 
-        near = far_first[::-1][: NZ // 2]
+        near = near_first[: NZ // 2]
         for d in near:
             res_copy(k, b, d).wait_recv()
         total = term(0)
         for d in near:
             total = total + term(d)
-        for d in far_first[::-1][NZ // 2 :]:
+        for d in near_first[NZ // 2 :]:
             res_copy(k, b, d).wait_recv()
-        for d in far_first[::-1][NZ // 2 :]:
+        for d in near_first[NZ // 2 :]:
             total = total + term(d)
         tin[k, x, at, :] = total
         for d in range(1, NX):
@@ -260,12 +260,12 @@
             else:
                 tile = maps[carry_kind, n + (1 if backward else 0)]
                 eout[k, spot(k, b, n), :] = eout[k, spot(k, b, n), :] + times(carry, tile)
-        for d in far_first:
+        for d in near_first:
             e_copy(k, b, d).start()
         ein[k, spot(k, b, z), :] = eout[k, spot(k, b, z), :]
 
     def arrive(k, b):
-        for d in far_first[::-1]:
+        for d in near_first:
             e_copy(k, b, d).wait_recv()
 
     def relax(k, b, ahead, old):

time: 147 us -> 153 us (1.041)
  Pallas kernels: 141 us -> 147 us
    pallas_call x1, Pallas kernels: 141 us -> 147 us  [local(): pl.pallas_call(functools.partial(body, NX, NZ, NY, NC, factor), out_shape...]
where the time goes in v7:
time: 153 us
  Pallas kernels  147 us (96%)
  local copies, waits for them, and re-layouts  4.85 us (3%)
    pallas_call x1, Pallas kernels, local(): pl.pallas_call(functools.partial(body, NX, NZ, NY, NC, factor), out_shape...  147 us
    unnamed x5, local copies, waits for them, and re-layouts  4.85 us

profile of v7, /device:TPU:1, one launch (start us, length us, event | category | flops | bytes accessed | tf_op | source)
XLA Modules:
  0.0 152.8 jit_solution(13664844745207228498)
XLA Ops:
  0.6 147.3 %shard_map.67 = (f32[1024,128]{1,0:T(8,128)}, f32[1024,128]{1,0:T(8,128)}, f32[2,1152,128]{2,1,0:T(8,128)}) custom-call(f32[1024,128]{1,0:T(8,128)} %bitcast.11, f32[1024,128]{1,0:T(8,128)} %bitcast.12, bf16[2,1152,128]{2,1,0:T(8,128)(2,1)} %bitcast.10, f32[128,128]{1,0:T(8,128)} %bitcast.13), custom_call_target="tpu_custom_call" | custom-call | flops 5000000000 | bytes 5000000 | tf_op jit(solution)/shard_map/pallas_call | solution.py:583
  148.0 0.0 copy-start
  148.0 2.0 %copy.10 = f32[1,1,32,32,128]{4,3,2,1,0:T(8,128)} copy(f32[1,1,32,32,128]{4,3,2,1,0:T(8,128)} %bitcast.9) | data formatting | bytes 1048576
  150.0 1.9 %copy.11 = f32[1,1,32,32,128]{4,3,2,1,0:T(8,128)} copy(f32[1,1,32,32,128]{4,3,2,1,0:T(8,128)} %bitcast.8) | data formatting | bytes 1048576
  151.8 0.0 copy-done
  151.8 1.0 copy.12
Async XLA Ops:
  148.0 3.8 %copy-start = (f32[2,1152,128]{2,1,0:T(8,128)S(1)}, f32[2,1152,128]{2,1,0:T(8,128)}, u32[]{:S(2)}) copy-start(f32[2,1152,128]{2,1,0:T(8,128)} %get-tuple-element.8) | copy-start | bytes 3538948
